TPU v7x, 32 devices: a whole 2x2x4 slice. The times are simulated.
32 devices in a mesh: grp: 2 (over y), slab: 4 (over x, core), orb: 4 (over z).
Axes of the slice: x: 2, y: 2, z: 4, core: 2. Of those that a mesh axis runs over, the one named last changes fastest.
Arguments:
- mode_basis: bfloat16 [8, 5120, 256], P(('grp', 'slab'), 'orb'), parts along dimension 0, may hold values from -0.078125 to 0.078125
- onsite: bfloat16 [8, 2, 5120, 1280], P(('grp', 'slab'), None, 'orb'), parts along dimension 0, may hold values from -1.1953125 to 1.1953125
- onsite_cols: int32 [8, 32, 8], P(('grp', 'slab'), 'orb'), parts along dimension 0, may hold values from 0 to 31
- coupling: bfloat16 [8, 2, 5120, 1280], P(('grp', 'slab'), None, 'orb'), parts along dimension 0, may hold values from -0.29882812 to 0.29882812
- coupling_cols: int32 [8, 32, 8], P(('grp', 'slab'), 'orb'), parts along dimension 0, may hold values from 0 to 31
- energies: float32 [16], replicated, may hold values from -2 to 2
- owner: int32 [16], replicated, may hold values from 0 to 15, each once
Outputs:
- surface_gf: float32 [32, 2, 256, 256], P(('grp', 'slab', 'orb')), parts along dimension 0
- mode_dos: float32 [32, 4], P(('grp', 'slab', 'orb')), parts along dimension 0
There are 2 independent parts, one for each index of `grp`. A program takes and returns all parts, laid end to end along the dimension named above; an argument that names none is the same for every part. Nothing has to cross between parts.
Inputs may be any that keep to these rules, and one draw needn't show every extreme that they name: `owner`: each slot index appears once.
All inputs are finite; a program needn't handle non-finite values.
Results may differ from a plain program's by a relative error of at most 0.0003.
The roundings to bfloat16 on the way count: a program that leaves them out, or rounds other values in their place, can miss the bound.
Values may be sent and summed in bfloat16 or wider, within the bound.
A program may use at most 128 MiB of HBM per device.

v0:
```python
import jax
import jax.numpy as jnp
from jax import lax
from jax.sharding import PartitionSpec as P

M = 256
BLK = 160
K = 8
NBLK = 32


broadening = 0.5
contact = 0.5


def shifted(array, axis, by):
    size = lax.axis_size(axis)
    return lax.ppermute(array, axis, [(i, (i + by) % size) for i in range(size)])


def matmul_exact(left, right):
    return jnp.matmul(left, right, precision=lax.Precision.HIGHEST)


def transpose_last(value):
    return jnp.swapaxes(value, -1, -2)


def complex_product(left_factor_real, left_factor_imaginary, right_re, right_im):
    real = matmul_exact(left_factor_real, right_re) - matmul_exact(left_factor_imaginary, right_im)
    imag = matmul_exact(left_factor_real, right_im) + matmul_exact(left_factor_imaginary, right_re)
    return (real, imag)


def adjoint_product(left_factor_real, left_factor_imaginary, right_re, right_im):
    real = matmul_exact(transpose_last(left_factor_real), right_re) + matmul_exact(
        transpose_last(left_factor_imaginary), right_im
    )
    imag = matmul_exact(transpose_last(left_factor_real), right_im) - matmul_exact(
        transpose_last(left_factor_imaginary), right_re
    )
    return (real, imag)


def invert(real, imag):
    gram_re, gram_im = adjoint_product(real, imag, real, imag)
    upper = jnp.concatenate([gram_re, -gram_im], -1)
    bottom = jnp.concatenate([gram_im, gram_re], -1)
    system = jnp.concatenate([upper, bottom], -2)
    factor = jnp.linalg.cholesky(system)
    rhs = jnp.concatenate([transpose_last(real), -transpose_last(imag)], -2)
    middle = lax.linalg.triangular_solve(factor, rhs, left_side=True, lower=True)
    result = lax.linalg.triangular_solve(
        factor, middle, left_side=True, lower=True, transpose_a=True
    )
    order = real.shape[-1]
    return (result[..., :order, :], result[..., order:, :])


def sweep(energy, blocks):
    order = blocks.shape[-1]
    ident = jnp.eye(order, dtype=blocks.dtype)
    shift_re = energy[:, None, None] * ident
    shift_im = broadening * ident
    wide_re, wide_im = adjoint_product(blocks[-1, 2], blocks[-1, 3], blocks[-1, 2], blocks[-1, 3])
    first_re = shift_re - blocks[0, 0] - contact * wide_im
    leading_imaginary = jnp.broadcast_to(
        shift_im - blocks[0, 1] + contact * wide_re, first_re.shape
    )
    green_re, green_im = invert(first_re, leading_imaginary)
    first_dos = -jnp.trace(green_im, axis1=-2, axis2=-1) / order

    def advance(carry, partial_blocks):
        prev_re, prev_im = carry
        hamil, hopping_coupling_matrix = partial_blocks
        prod_re, prod_im = complex_product(
            prev_re, prev_im, hopping_coupling_matrix[0], hopping_coupling_matrix[1]
        )
        self_re, self_im = adjoint_product(
            hopping_coupling_matrix[0], hopping_coupling_matrix[1], prod_re, prod_im
        )
        next_re, next_im = invert(shift_re - hamil[0] - self_re, shift_im - hamil[1] - self_im)
        return ((next_re, next_im), -jnp.trace(next_im, axis1=-2, axis2=-1) / order)

    (green_re, green_im), rest = lax.scan(
        advance, (green_re, green_im), (blocks[1:, :2], blocks[:-1, 2:])
    )
    dos = jnp.concatenate([first_dos[None], rest], 0)
    return (jnp.stack([green_re, green_im], 1), jnp.transpose(dos))


def hermitian_blocks(raw):
    real = (raw[:, 0] + transpose_last(raw[:, 0])) / 2.0
    imag = (raw[:, 1] - transpose_last(raw[:, 1])) / 2.0
    return jnp.stack([real, imag, raw[:, 2], raw[:, 3]], 1)


def pick_blocks(table, index):
    return table[index]


def project(hamil, columns, mode_basis_row_block, basis_cols):
    slab_count = hamil.shape[0]
    row_count = hamil.shape[2]
    block_count = columns.shape[1]
    table = basis_cols.reshape(slab_count, NBLK, BLK, M)
    chosen = jax.vmap(pick_blocks)(table, columns).reshape(slab_count, block_count, K * BLK, M)
    shaped = hamil.reshape(slab_count, 2, block_count, BLK, K * BLK)
    matrix_product_result = jnp.einsum(
        "scbrk,sbkm->scbrm", shaped, chosen, preferred_element_type=jnp.float32
    )
    matrix_product_result = matrix_product_result.astype(jnp.bfloat16).reshape(
        slab_count, 2, row_count, M
    )
    return jnp.einsum(
        "atw,abti->abwi",
        mode_basis_row_block,
        matrix_product_result,
        preferred_element_type=jnp.float32,
    )


def on_device(mode_basis, onsite, onsite_cols, coupling, coupling_cols, energies, owner):
    slab_count = mode_basis.shape[0]
    own_all = lax.all_gather(mode_basis, "orb", axis=1, tiled=True)
    moved_rows = shifted(mode_basis, "slab", -1)
    first_next = lax.all_gather(moved_rows, "orb", axis=1, tiled=True)
    next_all = jnp.concatenate([own_all[1:], first_next], 0)
    onsite_part = project(onsite, onsite_cols, mode_basis, own_all)
    coupling_part = project(coupling, coupling_cols, mode_basis, next_all)
    partial_value = jnp.concatenate([onsite_part, coupling_part], 1).reshape(slab_count, 4 * M * M)
    summed = lax.psum(partial_value, "orb")
    collected = lax.all_gather(summed, "slab", axis=0, tiled=True)
    blocks = hermitian_blocks(collected.reshape(-1, 4, M, M))
    energy_count = energies.shape[0]
    per_device = energy_count // lax.axis_size(("slab", "orb"))
    slot_index = lax.axis_index(("slab", "orb")) * per_device + jnp.arange(
        per_device, dtype=jnp.int32
    )
    positions = jnp.arange(energy_count, dtype=jnp.int32)
    selected_owner_device = jnp.sum(
        jnp.where(positions[None, :] == slot_index[:, None], owner[None, :], 0), 1
    )
    slot_energy = jnp.sum(
        jnp.where(positions[None, :] == selected_owner_device[:, None], energies[None, :], 0.0), 1
    )
    green, dos = sweep(slot_energy, blocks)
    return (green, dos)


def solution(mesh):
    in_specs = (
        P(("grp", "slab"), "orb", None),
        P(("grp", "slab"), None, "orb", None),
        P(("grp", "slab"), "orb", None),
        P(("grp", "slab"), None, "orb", None),
        P(("grp", "slab"), "orb", None),
        P(),
        P(),
    )
    out_specs = (P(("grp", "slab", "orb"), None, None, None), P(("grp", "slab", "orb"), None))
    return jax.shard_map(
        on_device, mesh=mesh, in_specs=in_specs, out_specs=out_specs, check_vma=False
    )
```

profile of v0, /device:TPU:0, one launch (start us, length us, event | category | flops | bytes accessed | tf_op | source)
XLA Modules:
  0.0 925.2 jit_solution(16845355378103504369)
XLA Ops:
  21.3 45.8 %all-gather.5.cloned.1.call-done = bf16[1,5120,256]{2,1,0:T(8,128)(2,1)} async-done(((bf16[1,1280,256]{2,1,0:T(8,128)(2,1)}), bf16[1,5120,256]{2,1,0:T(8,128)(2,1)}) %all-gather.5.cloned.1.call-update) | async-done | bytes 2621456 | tf_op jit(solution)/shard_map/all_gather | solution.py:125
  80.6 41.7 %all-gather.7.cloned.1.call-done = bf16[1,5120,256]{2,1,0:T(8,128)(2,1)} async-done(((bf16[1,1280,256]{2,1,0:T(8,128)(2,1)}), bf16[1,5120,256]{2,1,0:T(8,128)(2,1)}) %all-gather.7.cloned.1.call-update) | async-done | bytes 2621456 | tf_op jit(solution)/shard_map/all_gather | solution.py:127
  136.8 50.7 %all-reduce.3.cloned.1.call-done = f32[1,262144]{1,0:T(1,128)} async-done(((f32[1,262144]{1,0:T(1,128)}), f32[1,262144]{1,0:T(1,128)}) %all-reduce.3.cloned.1.call-update) | async-done | bytes 1048592 | tf_op jit(solution)/shard_map/psum | solution.py:132
  189.4 33.4 %all-gather.9.cloned.1.call-done = f32[4,1,262144]{2,1,0:T(1,128)} async-done(((f32[1,1,262144]{2,1,0:T(1,128)}), f32[4,1,262144]{2,1,0:T(1,128)}) %all-gather.9.cloned.1.call-update) | async-done | bytes 4194320 | tf_op jit(solution)/shard_map/all_gather | solution.py:133
  222.8 14.8 %reduce.34 = f32[4,262144]{1,0:T(4,128)} reduce(f32[4,1,262144]{2,1,0:T(1,128)} %all-gather.9.cloned.1.call-done, f32[]{:T(128)} %constant.247), dimensions={1}, to_apply=%all-gather.reduce_sub_computation | reduce | bytes 8388612 | tf_op jit(solution)/shard_map/all_gather | solution.py:133
  257.9 11.7 %custom-call.52 = f32[1,128,128]{2,1,0:T(8,128)S(1)} custom-call(f32[1,128,128]{2,1,0:T(8,128)S(1)} %cholesky.438), custom_call_target="Cholesky" | custom-call | tf_op jit(solution)/shard_map/jit(cholesky)/cholesky | solution.py:50
  307.9 13.3 %custom-call.56 = f32[1,128,128]{2,1,0:T(8,128)} custom-call(f32[1,128,128]{2,1,0:T(8,128)} %cholesky.447), custom_call_target="Cholesky" | custom-call | tf_op jit(solution)/shard_map/jit(cholesky)/cholesky | solution.py:50
  336.9 11.7 %custom-call.58 = f32[1,128,128]{2,1,0:T(8,128)S(1)} custom-call(f32[1,128,128]{2,1,0:T(8,128)S(1)} %fusion.107), custom_call_target="Cholesky" | custom-call | tf_op jit(solution)/shard_map/jit(cholesky)/cholesky | solution.py:50
  353.6 13.8 %while.26 = (s32[]{:T(128)}, f32[1,512,512]{2,1,0:T(8,128)}, s32[4,2]{0,1:T(2,128)S(1)}, f32[4,1,128,128]{3,2,1,0:T(8,128)}, s32[]{:T(128)}) while((s32[]{:T(128)}, f32[1,512,512]{2,1,0:T(8,128)}, s32[4,2]{0,1:T(2,128)S(1)}, f32[4,1,128,128]{3,2,1,0:T(8,128)}, s32[]{:T(128)}) %tuple.112), condition=%wide.while_cond.1.clone, body=%wide.while_body.1.clone.sunk | while | flops 2 | bytes 132705 | solution.py:53
  367.4 40.4 %custom-call.60 = f32[1,4,128,128]{2,3,1,0:T(8,128)S(1)} custom-call(f32[1,4,128,128]{3,2,1,0:T(8,128)} %bitcast.869), custom_call_target="InvertDiagBlocksLowerTriangular" | custom-call | tf_op jit(solution)/shard_map/triangular_solve/custom-call.8 | solution.py:53
  422.5 493.8 %while.25 = (s32[]{:T(128)}, f32[1,256,256]{2,1,0:T(8,128)S(1)}, f32[1,256,256]{2,1,0:T(8,128)S(1)}, f32[3,1]{0,1:T(1,128)S(1)}, f32[3,2,256,256]{2,3,0,1:T(8,12...) while((s32[]{:T(128)}, f32[1,256,256]{2,1,0:T(8,128)S(1)}, ...), condition=%wide.region_13.17_spmd.clone, body=%wide.region_11.16_spmd.clone.sunk | while | flops 3830776832 | bytes 38675400 | solution.py:85
  486.8 11.7 %custom-call.75 = f32[1,128,128]{2,1,0:T(8,128)S(1)} custom-call(f32[1,128,128]{2,1,0:T(8,128)S(1)} %cholesky.772), custom_call_target="Cholesky" | custom-call | tf_op jit(solution)/shard_map/while/body/eval_jaxpr/jit(cholesky)/cholesky | solution.py:50
  511.9 11.7 %custom-call.77 = f32[1,128,128]{2,1,0:T(8,128)S(1)} custom-call(f32[1,128,128]{2,1,0:T(8,128)S(1)} %cholesky.773), custom_call_target="Cholesky" | custom-call | tf_op jit(solution)/shard_map/while/body/eval_jaxpr/jit(cholesky)/cholesky | solution.py:50
  536.2 11.7 %custom-call.79 = f32[1,128,128]{2,1,0:T(8,128)S(1)} custom-call(f32[1,128,128]{2,1,0:T(8,128)S(1)} %fusion.288), custom_call_target="Cholesky" | custom-call | tf_op jit(solution)/shard_map/while/body/eval_jaxpr/jit(cholesky)/cholesky | solution.py:50
  557.5 39.3 %custom-call.81 = f32[1,4,128,128]{2,3,1,0:T(8,128)S(1)} custom-call(f32[1,4,128,128]{3,2,1,0:T(8,128)S(1)} %bitcast.870), custom_call_target="InvertDiagBlocksLowerTriangular" | custom-call | tf_op jit(solution)/shard_map/while/body/eval_jaxpr/triangular_solve/custom-call.8 | solution.py:53
  619.3 11.7 %custom-call.73 = f32[1,128,128]{2,1,0:T(8,128)S(1)} custom-call(f32[1,128,128]{2,1,0:T(8,128)S(1)} %cholesky.770), custom_call_target="Cholesky" | custom-call | tf_op jit(solution)/shard_map/while/body/eval_jaxpr/jit(cholesky)/cholesky | solution.py:50
  643.6 11.7 %custom-call.75 = f32[1,128,128]{2,1,0:T(8,128)S(1)} custom-call(f32[1,128,128]{2,1,0:T(8,128)S(1)} %cholesky.772), custom_call_target="Cholesky" | custom-call | tf_op jit(solution)/shard_map/while/body/eval_jaxpr/jit(cholesky)/cholesky | solution.py:50
  668.7 11.7 %custom-call.77 = f32[1,128,128]{2,1,0:T(8,128)S(1)} custom-call(f32[1,128,128]{2,1,0:T(8,128)S(1)} %cholesky.773), custom_call_target="Cholesky" | custom-call | tf_op jit(solution)/shard_map/while/body/eval_jaxpr/jit(cholesky)/cholesky | solution.py:50
  692.9 11.7 %custom-call.79 = f32[1,128,128]{2,1,0:T(8,128)S(1)} custom-call(f32[1,128,128]{2,1,0:T(8,128)S(1)} %fusion.288), custom_call_target="Cholesky" | custom-call | tf_op jit(solution)/shard_map/while/body/eval_jaxpr/jit(cholesky)/cholesky | solution.py:50
  714.2 39.3 %custom-call.81 = f32[1,4,128,128]{2,3,1,0:T(8,128)S(1)} custom-call(f32[1,4,128,128]{3,2,1,0:T(8,128)S(1)} %bitcast.870), custom_call_target="InvertDiagBlocksLowerTriangular" | custom-call | tf_op jit(solution)/shard_map/while/body/eval_jaxpr/triangular_solve/custom-call.8 | solution.py:53
  800.3 11.7 %custom-call.75 = f32[1,128,128]{2,1,0:T(8,128)S(1)} custom-call(f32[1,128,128]{2,1,0:T(8,128)S(1)} %cholesky.772), custom_call_target="Cholesky" | custom-call | tf_op jit(solution)/shard_map/while/body/eval_jaxpr/jit(cholesky)/cholesky | solution.py:50
  825.4 11.7 %custom-call.77 = f32[1,128,128]{2,1,0:T(8,128)S(1)} custom-call(f32[1,128,128]{2,1,0:T(8,128)S(1)} %cholesky.773), custom_call_target="Cholesky" | custom-call | tf_op jit(solution)/shard_map/while/body/eval_jaxpr/jit(cholesky)/cholesky | solution.py:50
  849.7 11.7 %custom-call.79 = f32[1,128,128]{2,1,0:T(8,128)S(1)} custom-call(f32[1,128,128]{2,1,0:T(8,128)S(1)} %fusion.288), custom_call_target="Cholesky" | custom-call | tf_op jit(solution)/shard_map/while/body/eval_jaxpr/jit(cholesky)/cholesky | solution.py:50
  871.0 39.3 %custom-call.81 = f32[1,4,128,128]{2,3,1,0:T(8,128)S(1)} custom-call(f32[1,4,128,128]{3,2,1,0:T(8,128)S(1)} %bitcast.870), custom_call_target="InvertDiagBlocksLowerTriangular" | custom-call | tf_op jit(solution)/shard_map/while/body/eval_jaxpr/triangular_solve/custom-call.8 | solution.py:53
  (353 shorter events, 398.6 us)
Async XLA Ops:
  7.2 59.9 %all-gather.5.cloned.1.call-start = ((), (), s32[]{:S(2)}) async-start(), calls=%async_computation | async-start | bytes 3276800 | tf_op jit(solution)/shard_map/all_gather | solution.py:125
  7.9 114.4 %all-gather.7.cloned.1.call-start = ((), (), s32[]{:S(2)}) async-start(), calls=%async_computation.1 | async-start | bytes 3276800 | tf_op jit(solution)/shard_map/all_gather | solution.py:127
  7.9 10.8 %collective-permute-start = (bf16[1,1280,256]{2,1,0:T(8,128)(2,1)}, bf16[1,1280,256]{2,1,0:T(8,128)(2,1)S(1)}, u32[]{:S(2)}, u32[]{:S(2)}) collective-permute-start(bf16[1,1280,256]{2,1,0:T(8,128)(2,1)} %param.14), channel_id=1, source_target_pairs={{0,12},{4,0},{8,4},{12,8},{1,13},{5,1},{9,5},{13,9},{2,14},{6,2},{... | collective-permute-start | bytes 1966088 | tf_op jit(solution)/shard_map/ppermute | solution.py:18
  18.8 0.9 copy-start.11
  19.7 167.8 %all-reduce.3.cloned.1.call-start = ((), (), s32[]{:S(2)}) async-start(), calls=%async_computation.2 | async-start | bytes 2097152 | tf_op jit(solution)/shard_map/psum | solution.py:132
  78.9 1.1 copy-start.10
  134.6 52.9 %copy-start.12 = (s32[16]{0:T(128)S(1)}, s32[16]{0:T(128)}, u32[]{:S(2)}) copy-start(s32[16]{0:T(128)} %param.20) | copy-start | bytes 196
  134.6 53.6 %copy-start.13 = (f32[16]{0:T(128)S(1)}, f32[16]{0:T(128)}, u32[]{:S(2)}) copy-start(f32[16]{0:T(128)} %param.19) | copy-start | bytes 196
  136.7 86.1 %all-gather.9.cloned.1.call-start = ((), (), s32[]{:S(2)}) async-start(), calls=%async_computation.3 | async-start | bytes 5242880 | tf_op jit(solution)/shard_map/all_gather | solution.py:133
  240.6 3.2 copy-start.1
  245.5 2.2 copy-start.6
  245.5 4.9 copy-start.8
  253.6 0.7 copy-start.2
  253.7 0.8 copy-start.4
  254.1 0.7 copy-start.5
  257.9 11.7 %copy-start.3 = (f32[1,512,512]{2,1,0:T(8,128)}, f32[1,512,512]{2,1,0:T(8,128)S(1)}, u32[]{:S(2)}) copy-start(f32[1,512,512]{2,1,0:T(8,128)S(1)} %fusion.110) | copy-start | bytes 3145732
  282.5 0.7 copy-start.9
  353.6 57.6 %copy-start.7 = (f32[1,256,256]{2,1,0:T(8,128)S(1)}, f32[1,256,256]{2,1,0:T(8,128)}, u32[]{:S(2)}) copy-start(f32[1,256,256]{2,1,0:T(8,128)} %get-tuple-element.193) | copy-start | bytes 786436
  461.7 1.0 copy-start
  618.4 1.0 copy-start
  775.1 1.0 copy-start
Sparse Core Ops, SparseCore 0:
  9.6 57.4 all-gather.4
  68.7 53.5 all-gather.6
  136.8 50.5 all-reduce.2
  188.9 33.8 all-gather.8
where the time goes:
time: 935 us; the launch traced here: 925 us
  other arithmetic  507 us (54%)
  waiting for transfers between devices  181 us (19%)
  matrix products  112 us (12%)
  local copies, waits for them, and re-layouts  71 us (8%)
  loops' own time  34.3 us (4%)
  between operations  17.8 us (2%)
    another operation x56, other arithmetic, invert(): factor = jnp.linalg.cholesky(system)  319 us
    another operation x20, other arithmetic, invert(): lax.linalg.triangular_solve(factor, middle, left_side=True, lower=True, t...  160 us
    dot_general x44, matrix products, matmul_exact(): return jnp.matmul(left, right, precision=lax.Precision.HIGHEST)  50.9 us
    psum x1, waiting for transfers between devices, on_device(): summed = lax.psum(partial_value, 'orb')  50.7 us
    all_gather x1, waiting for transfers between devices, on_device(): own_all = lax.all_gather(mode_basis, 'orb', axis=1, tiled=True)  45.8 us
    all_gather x1, waiting for transfers between devices, on_device(): first_next = lax.all_gather(moved_rows, 'orb', axis=1, tiled=True)  41.7 us
    another operation x52, local copies, waits for them, and re-layouts, invert(): lax.linalg.triangular_solve(factor, middle, left_side=True, lower=True, t...  37.7 us
    another operation x1, loops' own time, sweep(): lax.scan(advance, (green_re, green_im), (blocks[1:, :2], blocks[:-1, 2:]))  34 us
  transfers between devices with their start and end apart: 5, of which 5 were waited for; matrix products, arithmetic and copies ran while one was open for 2% of the time, Pallas kernels for 0%

commit v1 on v0

v1 whole, which is shorter than its diff:
```python
import jax
import jax.numpy as jnp
from jax import lax
from jax.experimental import pallas as pl
from jax.experimental.pallas import tpu as pltpu
from jax.sharding import PartitionSpec as P

M = 256
BLK = 160
K = 8
NBLK = 32


broadening = 0.5
contact = 0.5


def shifted(array, axis, by):
    size = lax.axis_size(axis)
    return lax.ppermute(array, axis, [(i, (i + by) % size) for i in range(size)])


HALF = 128
TILES = HALF // 8


def spread(tile, index):
    return jnp.take_along_axis(tile, index, axis=1, mode="promise_in_bounds")


def invert_half(re, im):
    lane = lax.broadcasted_iota(jnp.int32, (8, HALF), 1)
    sub = lax.broadcasted_iota(jnp.int32, (8, HALF), 0)

    def block_step(block, _):
        first = block * 8
        rows_re, rows_im = re[block], im[block]
        for j in range(8):
            index = jnp.full((8, HALF), first + j, jnp.int32)
            at = lane == index
            col_re, col_im = spread(rows_re, index), spread(rows_im, index)
            row_re = jnp.broadcast_to(rows_re[j : j + 1], (8, HALF))
            row_im = jnp.broadcast_to(rows_im[j : j + 1], (8, HALF))
            piv_re = jnp.broadcast_to(col_re[j : j + 1], (8, HALF))
            piv_im = jnp.broadcast_to(col_im[j : j + 1], (8, HALF))
            scale = 1.0 / (piv_re * piv_re + piv_im * piv_im)
            inv_re, inv_im = piv_re * scale, -piv_im * scale
            row_re, row_im = jnp.where(at, 1.0, row_re), jnp.where(at, 0.0, row_im)
            new_re = row_re * inv_re - row_im * inv_im
            new_im = row_re * inv_im + row_im * inv_re
            rest_re = jnp.where(at, 0.0, rows_re) - (col_re * new_re - col_im * new_im)
            rest_im = jnp.where(at, 0.0, rows_im) - (col_re * new_im + col_im * new_re)
            rows_re = jnp.where(sub == j, new_re, rest_re)
            rows_im = jnp.where(sub == j, new_im, rest_im)
        inside = (lane >= first) & (lane < first + 8)
        for half in range(2):
            ids = range(half * 8, half * 8 + 8)
            old = [(re[t], im[t]) for t in ids]
            acc = [(jnp.where(inside, 0.0, a), jnp.where(inside, 0.0, b)) for a, b in old]
            for j in range(8):
                index = jnp.full((8, HALF), first + j, jnp.int32)
                row_re = jnp.broadcast_to(rows_re[j : j + 1], (8, HALF))
                row_im = jnp.broadcast_to(rows_im[j : j + 1], (8, HALF))
                for n in range(8):
                    col_re, col_im = spread(old[n][0], index), spread(old[n][1], index)
                    acc[n] = (
                        acc[n][0] - col_re * row_re + col_im * row_im,
                        acc[n][1] - col_re * row_im - col_im * row_re,
                    )
            for n, t in enumerate(ids):
                re[t], im[t] = acc[n]
        re[block], im[block] = rows_re, rows_im
        return 0

    lax.fori_loop(0, TILES, block_step, 0)


def exact(left, right):
    return lax.dot_general(
        left,
        right,
        (((1,), (0,)), ((), ())),
        precision=lax.Precision.HIGHEST,
        preferred_element_type=jnp.float32,
    )


def times(left, right):
    width = right[0].shape[1]
    wide = jnp.concatenate([left[0], left[1]], 1)
    table = jnp.concatenate(
        [
            jnp.concatenate([right[0], right[1]], 1),
            jnp.concatenate([-right[1], right[0]], 1),
        ],
        0,
    )
    out = exact(wide, table)
    return out[:, :width], out[:, width:]


def adjoint(value):
    return value[0].T, -value[1].T


def sweep_kernel(energy_ref, blocks_ref, green_ref, dos_ref, work_re, work_im):
    eye = lax.broadcasted_iota(jnp.int32, (M, M), 0) == lax.broadcasted_iota(jnp.int32, (M, M), 1)
    energy = energy_ref[0]

    def inverse_of_half(re, im):
        work_re[...] = re.reshape(TILES, 8, HALF)
        work_im[...] = im.reshape(TILES, 8, HALF)
        invert_half(work_re, work_im)
        return work_re[...].reshape(HALF, HALF), work_im[...].reshape(HALF, HALF)

    def store(rows, columns, value):
        green_ref[0, rows, columns] = value[0]
        green_ref[1, rows, columns] = value[1]

    def load(rows, columns):
        return green_ref[0, rows, columns], green_ref[1, rows, columns]

    low, high = slice(0, HALF), slice(HALF, M)

    def step(s, _):
        lead = s == 0
        hop = jnp.where(lead, blocks_ref.shape[0] - 1, s - 1)
        t = (blocks_ref[hop, 2], blocks_ref[hop, 3])
        t_adj = adjoint(t)

        @pl.when(lead)
        def _():
            wide = times(t_adj, t)
            green_ref[0] = contact * wide[1]
            green_ref[1] = -contact * wide[0]

        @pl.when(jnp.logical_not(lead))
        def _():
            self_energy = times(t_adj, times((green_ref[0], green_ref[1]), t))
            green_ref[0] = self_energy[0]
            green_ref[1] = self_energy[1]

        raw_re, raw_im = blocks_ref[s, 0], blocks_ref[s, 1]
        ham_re = (raw_re + raw_re.T) / 2.0
        ham_im = (raw_im - raw_im.T) / 2.0
        green_ref[0] = jnp.where(eye, energy, 0.0) - ham_re - green_ref[0]
        green_ref[1] = jnp.where(eye, broadening, 0.0) - ham_im - green_ref[1]

        corner = inverse_of_half(*load(low, low))
        store(low, low, corner)
        upper = times(corner, load(low, high))
        drop = times(load(high, low), upper)
        last = load(high, high)
        schur = inverse_of_half(last[0] - drop[0], last[1] - drop[1])
        corner = load(low, low)
        left = times(load(high, low), corner)
        bottom = times(schur, left)
        right = times(upper, schur)
        fill = times(upper, bottom)
        store(high, high, schur)
        store(high, low, (-bottom[0], -bottom[1]))
        store(low, high, (-right[0], -right[1]))
        store(low, low, (corner[0] + fill[0], corner[1] + fill[1]))
        dos_ref[s] = -jnp.sum(jnp.where(eye, green_ref[1], 0.0)) / M
        return 0

    lax.fori_loop(0, blocks_ref.shape[0], step, 0)


def sweep_one(energy, blocks):
    green, dos = pl.pallas_call(
        sweep_kernel,
        out_shape=(
            jax.ShapeDtypeStruct((2, M, M), jnp.float32),
            jax.ShapeDtypeStruct((blocks.shape[0],), jnp.float32),
        ),
        in_specs=[
            pl.BlockSpec(memory_space=pltpu.SMEM),
            pl.BlockSpec(memory_space=pltpu.VMEM),
        ],
        out_specs=(
            pl.BlockSpec(memory_space=pltpu.VMEM),
            pl.BlockSpec(memory_space=pltpu.SMEM),
        ),
        scratch_shapes=[pltpu.VMEM((TILES, 8, HALF), jnp.float32)] * 2,
        compiler_params=pltpu.CompilerParams(vmem_limit_bytes=40 * 1024 * 1024),
    )(energy.reshape(1), blocks)
    return green, dos


def sweep(energy, blocks):
    pairs = [sweep_one(energy[e], blocks) for e in range(energy.shape[0])]
    return jnp.stack([p[0] for p in pairs]), jnp.stack([p[1] for p in pairs])


def pick_blocks(table, index):
    return table[index]


def project(hamil, columns, mode_basis_row_block, basis_cols):
    slab_count = hamil.shape[0]
    row_count = hamil.shape[2]
    block_count = columns.shape[1]
    table = basis_cols.reshape(slab_count, NBLK, BLK, M)
    chosen = jax.vmap(pick_blocks)(table, columns).reshape(slab_count, block_count, K * BLK, M)
    shaped = hamil.reshape(slab_count, 2, block_count, BLK, K * BLK)
    matrix_product_result = jnp.einsum(
        "scbrk,sbkm->scbrm", shaped, chosen, preferred_element_type=jnp.float32
    )
    matrix_product_result = matrix_product_result.astype(jnp.bfloat16).reshape(
        slab_count, 2, row_count, M
    )
    return jnp.einsum(
        "atw,abti->abwi",
        mode_basis_row_block,
        matrix_product_result,
        preferred_element_type=jnp.float32,
    )


def on_device(mode_basis, onsite, onsite_cols, coupling, coupling_cols, energies, owner):
    slab_count = mode_basis.shape[0]
    own_all = lax.all_gather(mode_basis, "orb", axis=1, tiled=True)
    moved_rows = shifted(mode_basis, "slab", -1)
    first_next = lax.all_gather(moved_rows, "orb", axis=1, tiled=True)
    next_all = jnp.concatenate([own_all[1:], first_next], 0)
    onsite_part = project(onsite, onsite_cols, mode_basis, own_all)
    coupling_part = project(coupling, coupling_cols, mode_basis, next_all)
    partial_value = jnp.concatenate([onsite_part, coupling_part], 1).reshape(slab_count, 4 * M * M)
    summed = lax.psum(partial_value, "orb")
    collected = lax.all_gather(summed, "slab", axis=0, tiled=True)
    blocks = collected.reshape(-1, 4, M, M)
    energy_count = energies.shape[0]
    per_device = energy_count // lax.axis_size(("slab", "orb"))
    slot_index = lax.axis_index(("slab", "orb")) * per_device + jnp.arange(
        per_device, dtype=jnp.int32
    )
    positions = jnp.arange(energy_count, dtype=jnp.int32)
    selected_owner_device = jnp.sum(
        jnp.where(positions[None, :] == slot_index[:, None], owner[None, :], 0), 1
    )
    slot_energy = jnp.sum(
        jnp.where(positions[None, :] == selected_owner_device[:, None], energies[None, :], 0.0), 1
    )
    green, dos = sweep(slot_energy, blocks)
    return (green, dos)


def solution(mesh):
    in_specs = (
        P(("grp", "slab"), "orb", None),
        P(("grp", "slab"), None, "orb", None),
        P(("grp", "slab"), "orb", None),
        P(("grp", "slab"), None, "orb", None),
        P(("grp", "slab"), "orb", None),
        P(),
        P(),
    )
    out_specs = (P(("grp", "slab", "orb"), None, None, None), P(("grp", "slab", "orb"), None))
    return jax.shard_map(
        on_device, mesh=mesh, in_specs=in_specs, out_specs=out_specs, check_vma=False
    )
```

time: 935 us -> 376 us (0.40)
  other arithmetic: 507 us -> 18 us
  Pallas kernels: 0 us -> 128 us
  matrix products: 112 us -> 14.3 us
  local copies, waits for them, and re-layouts: 71 us -> 16.5 us
  loops' own time: 34.3 us -> 0 us
    another operation x79 -> x0, other arithmetic: 481 us -> none  [the longest x56 319 us: invert(): factor = jnp.linalg.cholesky(system)]
    pallas_call x0 -> x1, Pallas kernels: none -> 128 us  [sweep_one(): pl.pallas_call(sweep_kernel, out_shape=(jax.ShapeDtypeStruct((2, M, M), j...]
    dot_general x44 -> x0, matrix products: 50.9 us -> none  [matmul_exact(): return jnp.matmul(left, right, precision=lax.Precision.HIGHEST)]
    another operation x80 -> x0, matrix products: 46.6 us -> none  [the longest x24 23.6 us: invert(): factor = jnp.linalg.cholesky(system)]
    another operation x68 -> x0, local copies, waits for them, and re-layouts: 38.9 us -> none  [the longest x52 37.7 us: invert(): lax.linalg.triangular_solve(factor, middle, left_side=True, lower=True, t...]
    another operation x5 -> x0, loops' own time: 34.3 us -> none  [the longest x1 34 us: sweep(): lax.scan(advance, (green_re, green_im), (blocks[1:, :2], blocks[:-1, 2:]))]
  transfers between devices with their start and end apart: 5 -> 5, of which waited for: 5 -> 5; matrix products, arithmetic and copies ran while one was open for 2% -> 4% of each run, Pallas kernels for 0% -> 0%
where the time goes in v1:
time: 376 us; the launch traced here: 375 us
  waiting for transfers between devices  182 us (48%)
  Pallas kernels  128 us (34%)
  other arithmetic  18 us (5%)
  local copies, waits for them, and re-layouts  16.5 us (4%)
  matrix products  14.3 us (4%)
  between operations  13.9 us (4%)
    pallas_call x1, Pallas kernels, sweep_one(): pl.pallas_call(sweep_kernel, out_shape=(jax.ShapeDtypeStruct((2, M, M), j...  128 us
    psum x1, waiting for transfers between devices, on_device(): summed = lax.psum(partial_value, 'orb')  50.5 us
    all_gather x1, waiting for transfers between devices, on_device(): own_all = lax.all_gather(mode_basis, 'orb', axis=1, tiled=True)  45.8 us
    all_gather x1, waiting for transfers between devices, on_device(): first_next = lax.all_gather(moved_rows, 'orb', axis=1, tiled=True)  42.6 us
    all_gather x1, waiting for transfers between devices, on_device(): collected = lax.all_gather(summed, 'slab', axis=0, tiled=True)  33.4 us
    all_gather x1, other arithmetic, on_device(): collected = lax.all_gather(summed, 'slab', axis=0, tiled=True)  14.6 us
    dot_general x2, matrix products, project(): jnp.einsum('scbrk,sbkm->scbrm', shaped, chosen, preferred_element_type=jn...  13.2 us
    gather x6, local copies, waits for them, and re-layouts, pick_blocks(): return table[index]  10 us
  transfers between devices with their start and end apart: 5, of which 5 were waited for; matrix products, arithmetic and copies ran while one was open for 4% of the time, Pallas kernels for 0%

profile of v1, /device:TPU:0, one launch (start us, length us, event | category | flops | bytes accessed | tf_op | source)
XLA Modules:
  0.0 375.3 jit_solution(9336803790059107056)
XLA Ops:
  7.2 0.7 all-gather.5.cloned.1.call-update
  7.9 2.4 collective-permute-start
  10.4 8.4 %collective-permute-done = bf16[1,1280,256]{2,1,0:T(8,128)(2,1)S(1)} collective-permute-done((bf16[1,1280,256]{2,1,0:T(8,128)(2,1)}, bf16[1,1280,256]{2,1,0:T(8,128)(2,1)S(1)}, u32[]{:S(2)}, u32[]{:S(2)}) %collective-permute-start) | collective-permute-done | bytes 655392 | tf_op jit(solution)/shard_map/ppermute | solution.py:20
  18.8 0.8 copy-done.1
  19.7 0.7 fusion.19
  20.5 0.7 fusion.18
  21.3 45.8 %all-gather.5.cloned.1.call-done = bf16[1,5120,256]{2,1,0:T(8,128)(2,1)} async-done(((bf16[1,1280,256]{2,1,0:T(8,128)(2,1)}), bf16[1,5120,256]{2,1,0:T(8,128)(2,1)}) %all-gather.5.cloned.1.call-update) | async-done | bytes 2621456 | tf_op jit(solution)/shard_map/all_gather | solution.py:223
  67.1 4.9 %gather_fusion = bf16[64,160,256]{2,1,0:T(8,128)(2,1)} fusion(bf16[1,32,160,256]{3,2,1,0:T(8,128)(2,1)} %bitcast.66, s32[64]{0:T(128)S(1)} %reshape.84), kind=kCustom, calls=%fused_computation | custom fusion | bytes 10486272 | tf_op jit(solution)/shard_map/vmap()/gather | solution.py:197
  72.0 6.9 %fusion.13 = bf16[1,2,8,160,256]{4,3,1,2,0:T(8,128)(2,1)S(1)} fusion(bf16[8,1280,256,1]{2,1,3,0:T(8,128)(2,1)} %bitcast.68, bf16[2,8,160,1280]{3,2,1,0:T(8,128)(2,1)} %bitcast.75), kind=kOutput, calls=%fused_computation.9 | convolution fusion | flops 1678376960 | bytes 13107200 | tf_op jit(solution)/shard_map/scbrk,sbkm->scbrm/dot_general | solution.py:207
  79.1 0.5 convolution_bitcast_fusion.1
  79.6 42.6 %all-gather.7.cloned.1.call-done = bf16[1,5120,256]{2,1,0:T(8,128)(2,1)} async-done(((bf16[1,1280,256]{2,1,0:T(8,128)(2,1)}), bf16[1,5120,256]{2,1,0:T(8,128)(2,1)}) %all-gather.7.cloned.1.call-update) | async-done | bytes 2621456 | tf_op jit(solution)/shard_map/all_gather | solution.py:225
  122.3 4.9 %gather_fusion.1 = bf16[64,160,256]{2,1,0:T(8,128)(2,1)} fusion(bf16[1,32,160,256]{3,2,1,0:T(8,128)(2,1)} %bitcast.67, s32[64]{0:T(128)S(1)} %reshape.92), kind=kCustom, calls=%fused_computation.1 | custom fusion | bytes 10486272 | tf_op jit(solution)/shard_map/vmap()/gather | solution.py:197
  127.2 6.3 %fusion.10 = bf16[1,2,8,160,256]{4,3,1,2,0:T(8,128)(2,1)S(1)} fusion(bf16[8,1280,256,1]{2,1,3,0:T(8,128)(2,1)} %bitcast.69, bf16[2,8,160,1280]{3,2,1,0:T(8,128)(2,1)} %bitcast.76), kind=kOutput, calls=%fused_computation.8 | convolution fusion | flops 1678376960 | bytes 13107200 | tf_op jit(solution)/shard_map/scbrk,sbkm->scbrm/dot_general | solution.py:207
  133.6 0.5 convolution_bitcast_fusion
  134.3 0.3 copy.24
  134.6 2.1 copy.29
  136.7 0.2 all-gather.9.cloned.1.call-start
  136.9 50.5 %all-reduce.2.cloned.1.call-done = f32[1,262144]{1,0:T(1,128)} async-done(((f32[1,262144]{1,0:T(1,128)}), f32[1,262144]{1,0:T(1,128)}) %all-reduce.2.cloned.1.call-update) | async-done | bytes 1048592 | tf_op jit(solution)/shard_map/psum | solution.py:230
  187.5 0.6 fusion.26
  188.1 1.3 fusion.27
  189.4 33.4 %all-gather.9.cloned.1.call-done = f32[4,1,262144]{2,1,0:T(1,128)} async-done(((f32[1,1,262144]{2,1,0:T(1,128)}), f32[4,1,262144]{2,1,0:T(1,128)}) %all-gather.9.cloned.1.call-update) | async-done | bytes 4194320 | tf_op jit(solution)/shard_map/all_gather | solution.py:231
  222.8 14.6 %reduce.4 = f32[4,262144]{1,0:T(4,128)} reduce(f32[4,1,262144]{2,1,0:T(1,128)} %all-gather.9.cloned.1.call-done, f32[]{:T(128)} %constant.49), dimensions={1}, to_apply=%all-gather.reduce_sub_computation | reduce | bytes 8388612 | tf_op jit(solution)/shard_map/all_gather | solution.py:231
  237.4 3.0 copy.30
  240.4 128.3 %shard_map.86 = (f32[2,256,256]{2,1,0:T(8,128)}, f32[4]{0:T(128)}) custom-call(f32[1]{0:T(128)} %bitcast.energy_ref, f32[4,4,256,256]{3,2,1,0:T(8,128)S(1)} %bitcast.64), custom_call_target="tpu_custom_call" | custom-call | tf_op jit(solution)/shard_map/pallas_call | solution.py:171
  (22 shorter events, 0.6 us)
Async XLA Ops:
  7.2 59.9 %all-gather.5.cloned.1.call-start = ((), (), s32[]{:S(2)}) async-start(), calls=%async_computation | async-start | bytes 3276800 | tf_op jit(solution)/shard_map/all_gather | solution.py:223
  7.9 114.4 %all-gather.7.cloned.1.call-start = ((), (), s32[]{:S(2)}) async-start(), calls=%async_computation.1 | async-start | bytes 3276800 | tf_op jit(solution)/shard_map/all_gather | solution.py:225
  7.9 10.8 %collective-permute-start = (bf16[1,1280,256]{2,1,0:T(8,128)(2,1)}, bf16[1,1280,256]{2,1,0:T(8,128)(2,1)S(1)}, u32[]{:S(2)}, u32[]{:S(2)}) collective-permute-start(bf16[1,1280,256]{2,1,0:T(8,128)(2,1)} %param.7), channel_id=1, source_target_pairs={{0,12},{4,0},{8,4},{12,8},{1,13},{5,1},{9,5},{13,9},{2,14},{6,2},{... | collective-permute-start | bytes 1966088 | tf_op jit(solution)/shard_map/ppermute | solution.py:20
  18.8 0.8 copy-start.1
  19.7 167.8 %all-reduce.2.cloned.1.call-start = ((), (), s32[]{:S(2)}) async-start(), calls=%async_computation.2 | async-start | bytes 2097152 | tf_op jit(solution)/shard_map/psum | solution.py:230
  72.0 7.0 %copy-start = (bf16[1,1280,256]{2,1,0:T(8,128)(2,1)S(1)}, bf16[1,1280,256]{2,1,0:T(8,128)(2,1)}, u32[]{:S(2)}) copy-start(bf16[1,1280,256]{2,1,0:T(8,128)(2,1)} %param.7) | copy-start | bytes 1966084
  133.6 53.9 %copy-start.2 = (s32[16]{0:T(128)S(1)}, s32[16]{0:T(128)}, u32[]{:S(2)}) copy-start(s32[16]{0:T(128)} %param.13) | copy-start | bytes 196
  133.6 54.5 %copy-start.3 = (f32[16]{0:T(128)S(1)}, f32[16]{0:T(128)}, u32[]{:S(2)}) copy-start(f32[16]{0:T(128)} %param.12) | copy-start | bytes 196
  136.7 86.1 %all-gather.9.cloned.1.call-start = ((), (), s32[]{:S(2)}) async-start(), calls=%async_computation.3 | async-start | bytes 5242880 | tf_op jit(solution)/shard_map/all_gather | solution.py:231
Sparse Core Ops, SparseCore 0:
  9.6 57.4 all-gather.4
  68.7 53.5 all-gather.6
  136.8 50.5 all-reduce.1
  188.9 33.8 all-gather.8

commit v2 on v1

--- a/solution.py
+++ b/solution.py
@@ -32,47 +32,74 @@
     lane = lax.broadcasted_iota(jnp.int32, (8, HALF), 1)
     sub = lax.broadcasted_iota(jnp.int32, (8, HALF), 0)
 
-    def block_step(block, _):
-        first = block * 8
-        rows_re, rows_im = re[block], im[block]
+    def eliminate(first, rows_re, rows_im):
+        cols = []
         for j in range(8):
             index = jnp.full((8, HALF), first + j, jnp.int32)
-            at = lane == index
-            col_re, col_im = spread(rows_re, index), spread(rows_im, index)
+            cols.append((spread(rows_re, index), spread(rows_im, index)))
+        for j in range(8):
+            at = lane == first + j
+            here = sub == j
+            col_re, col_im = cols[j]
             row_re = jnp.broadcast_to(rows_re[j : j + 1], (8, HALF))
             row_im = jnp.broadcast_to(rows_im[j : j + 1], (8, HALF))
             piv_re = jnp.broadcast_to(col_re[j : j + 1], (8, HALF))
             piv_im = jnp.broadcast_to(col_im[j : j + 1], (8, HALF))
             scale = 1.0 / (piv_re * piv_re + piv_im * piv_im)
             inv_re, inv_im = piv_re * scale, -piv_im * scale
-            row_re, row_im = jnp.where(at, 1.0, row_re), jnp.where(at, 0.0, row_im)
-            new_re = row_re * inv_re - row_im * inv_im
-            new_im = row_re * inv_im + row_im * inv_re
-            rest_re = jnp.where(at, 0.0, rows_re) - (col_re * new_re - col_im * new_im)
-            rest_im = jnp.where(at, 0.0, rows_im) - (col_re * new_im + col_im * new_re)
-            rows_re = jnp.where(sub == j, new_re, rest_re)
-            rows_im = jnp.where(sub == j, new_im, rest_im)
+
+            def reduced(old_re, old_im, row_re, row_im):
+                new_re = row_re * inv_re - row_im * inv_im
+                new_im = row_re * inv_im + row_im * inv_re
+                rest_re = old_re - (col_re * new_re - col_im * new_im)
+                rest_im = old_im - (col_re * new_im + col_im * new_re)
+                return jnp.where(here, new_re, rest_re), jnp.where(here, new_im, rest_im)
+
+            for m in range(j + 1, 8):
+                old_re, old_im = cols[m]
+                cols[m] = reduced(
+                    old_re,
+                    old_im,
+                    jnp.broadcast_to(old_re[j : j + 1], (8, HALF)),
+                    jnp.broadcast_to(old_im[j : j + 1], (8, HALF)),
+                )
+            rows_re, rows_im = reduced(
+                jnp.where(at, 0.0, rows_re),
+                jnp.where(at, 0.0, rows_im),
+                jnp.where(at, 1.0, row_re),
+                jnp.where(at, 0.0, row_im),
+            )
+        return rows_re, rows_im
+
+    def update(first, old, panel):
         inside = (lane >= first) & (lane < first + 8)
-        for half in range(2):
-            ids = range(half * 8, half * 8 + 8)
-            old = [(re[t], im[t]) for t in ids]
-            acc = [(jnp.where(inside, 0.0, a), jnp.where(inside, 0.0, b)) for a, b in old]
-            for j in range(8):
-                index = jnp.full((8, HALF), first + j, jnp.int32)
-                row_re = jnp.broadcast_to(rows_re[j : j + 1], (8, HALF))
-                row_im = jnp.broadcast_to(rows_im[j : j + 1], (8, HALF))
-                for n in range(8):
-                    col_re, col_im = spread(old[n][0], index), spread(old[n][1], index)
-                    acc[n] = (
-                        acc[n][0] - col_re * row_re + col_im * row_im,
-                        acc[n][1] - col_re * row_im - col_im * row_re,
-                    )
+        acc = [(jnp.where(inside, 0.0, a), jnp.where(inside, 0.0, b)) for a, b in old]
+        for j in range(8):
+            index = jnp.full((8, HALF), first + j, jnp.int32)
+            row_re = jnp.broadcast_to(panel[0][j : j + 1], (8, HALF))
+            row_im = jnp.broadcast_to(panel[1][j : j + 1], (8, HALF))
+            for n in range(len(old)):
+                col_re, col_im = spread(old[n][0], index), spread(old[n][1], index)
+                acc[n] = (
+                    acc[n][0] - col_re * row_re + col_im * row_im,
+                    acc[n][1] - col_re * row_im - col_im * row_re,
+                )
+        return acc
+
+    def block_step(block, panel):
+        first = block * 8
+        after = jnp.minimum(block + 1, TILES - 1)
+        ahead = update(first, [(re[after], im[after])], panel)[0]
+        following = eliminate(after * 8, *ahead)
+        for part in range(0, TILES, 8):
+            ids = range(part, part + 8)
+            fresh = update(first, [(re[t], im[t]) for t in ids], panel)
             for n, t in enumerate(ids):
-                re[t], im[t] = acc[n]
-        re[block], im[block] = rows_re, rows_im
-        return 0
-
-    lax.fori_loop(0, TILES, block_step, 0)
+                re[t], im[t] = fresh[n]
+        re[block], im[block] = panel
+        return following
+
+    lax.fori_loop(0, TILES, block_step, eliminate(0, re[0], im[0]))
 
 
 def exact(left, right):
@@ -103,7 +130,7 @@
     return value[0].T, -value[1].T
 
 
-def sweep_kernel(energy_ref, blocks_ref, green_ref, dos_ref, work_re, work_im):
+def sweep_kernel(energy_ref, hamil_ref, hopping_ref, green_ref, dos_ref, work_re, work_im):
     eye = lax.broadcasted_iota(jnp.int32, (M, M), 0) == lax.broadcasted_iota(jnp.int32, (M, M), 1)
     energy = energy_ref[0]
 
@@ -124,8 +151,8 @@
 
     def step(s, _):
         lead = s == 0
-        hop = jnp.where(lead, blocks_ref.shape[0] - 1, s - 1)
-        t = (blocks_ref[hop, 2], blocks_ref[hop, 3])
+        hop = jnp.where(lead, hamil_ref.shape[0] - 1, s - 1)
+        t = (hopping_ref[hop, 0], hopping_ref[hop, 1])
         t_adj = adjoint(t)
 
         @pl.when(lead)
@@ -140,7 +167,7 @@
             green_ref[0] = self_energy[0]
             green_ref[1] = self_energy[1]
 
-        raw_re, raw_im = blocks_ref[s, 0], blocks_ref[s, 1]
+        raw_re, raw_im = hamil_ref[s, 0], hamil_ref[s, 1]
         ham_re = (raw_re + raw_re.T) / 2.0
         ham_im = (raw_im - raw_im.T) / 2.0
         green_ref[0] = jnp.where(eye, energy, 0.0) - ham_re - green_ref[0]
@@ -164,18 +191,19 @@
         dos_ref[s] = -jnp.sum(jnp.where(eye, green_ref[1], 0.0)) / M
         return 0
 
-    lax.fori_loop(0, blocks_ref.shape[0], step, 0)
-
-
-def sweep_one(energy, blocks):
+    lax.fori_loop(0, hamil_ref.shape[0], step, 0)
+
+
+def sweep_one(energy, hamil, hopping):
     green, dos = pl.pallas_call(
         sweep_kernel,
         out_shape=(
             jax.ShapeDtypeStruct((2, M, M), jnp.float32),
-            jax.ShapeDtypeStruct((blocks.shape[0],), jnp.float32),
+            jax.ShapeDtypeStruct((hamil.shape[0],), jnp.float32),
         ),
         in_specs=[
             pl.BlockSpec(memory_space=pltpu.SMEM),
+            pl.BlockSpec(memory_space=pltpu.VMEM),
             pl.BlockSpec(memory_space=pltpu.VMEM),
         ],
         out_specs=(
@@ -184,12 +212,12 @@
         ),
         scratch_shapes=[pltpu.VMEM((TILES, 8, HALF), jnp.float32)] * 2,
         compiler_params=pltpu.CompilerParams(vmem_limit_bytes=40 * 1024 * 1024),
-    )(energy.reshape(1), blocks)
+    )(energy.reshape(1), hamil, hopping)
     return green, dos
 
 
-def sweep(energy, blocks):
-    pairs = [sweep_one(energy[e], blocks) for e in range(energy.shape[0])]
+def sweep(energy, hamil, hopping):
+    pairs = [sweep_one(energy[e], hamil, hopping) for e in range(energy.shape[0])]
     return jnp.stack([p[0] for p in pairs]), jnp.stack([p[1] for p in pairs])
 
 
@@ -201,14 +229,15 @@
     slab_count = hamil.shape[0]
     row_count = hamil.shape[2]
     block_count = columns.shape[1]
-    table = basis_cols.reshape(slab_count, NBLK, BLK, M)
-    chosen = jax.vmap(pick_blocks)(table, columns).reshape(slab_count, block_count, K * BLK, M)
+    width = basis_cols.shape[2]
+    table = basis_cols.reshape(slab_count, NBLK, BLK, width)
+    chosen = jax.vmap(pick_blocks)(table, columns).reshape(slab_count, block_count, K * BLK, width)
     shaped = hamil.reshape(slab_count, 2, block_count, BLK, K * BLK)
     matrix_product_result = jnp.einsum(
         "scbrk,sbkm->scbrm", shaped, chosen, preferred_element_type=jnp.float32
     )
     matrix_product_result = matrix_product_result.astype(jnp.bfloat16).reshape(
-        slab_count, 2, row_count, M
+        slab_count, 2, row_count, width
     )
     return jnp.einsum(
         "atw,abti->abwi",
@@ -218,18 +247,29 @@
     )
 
 
+def share(partial_value):
+    slab_count = partial_value.shape[0]
+    rows = partial_value.reshape(slab_count, 2 * M, M)
+    own = lax.psum_scatter(rows, "orb", scatter_dimension=1, tiled=True)
+    every = lax.all_gather(own, ("slab", "orb"), axis=0, tiled=False)
+    every = every.reshape(lax.axis_size("slab"), lax.axis_size("orb"), slab_count, -1, M)
+    return jnp.swapaxes(every, 1, 2).reshape(-1, 2, M, M)
+
+
 def on_device(mode_basis, onsite, onsite_cols, coupling, coupling_cols, energies, owner):
-    slab_count = mode_basis.shape[0]
-    own_all = lax.all_gather(mode_basis, "orb", axis=1, tiled=True)
-    moved_rows = shifted(mode_basis, "slab", -1)
-    first_next = lax.all_gather(moved_rows, "orb", axis=1, tiled=True)
-    next_all = jnp.concatenate([own_all[1:], first_next], 0)
-    onsite_part = project(onsite, onsite_cols, mode_basis, own_all)
-    coupling_part = project(coupling, coupling_cols, mode_basis, next_all)
-    partial_value = jnp.concatenate([onsite_part, coupling_part], 1).reshape(slab_count, 4 * M * M)
-    summed = lax.psum(partial_value, "orb")
-    collected = lax.all_gather(summed, "slab", axis=0, tiled=True)
-    blocks = collected.reshape(-1, 4, M, M)
+    halves = [mode_basis[:, :, : M // 2], mode_basis[:, :, M // 2 :]]
+    own = [lax.all_gather(half, "orb", axis=1, tiled=True) for half in halves]
+    following = [
+        jnp.concatenate([all_rows[1:], shifted(all_rows[:1], "slab", -1)], 0) for all_rows in own
+    ]
+    onsite_part = jnp.concatenate(
+        [project(onsite, onsite_cols, mode_basis, half) for half in own], -1
+    )
+    hamil = share(onsite_part)
+    coupling_part = jnp.concatenate(
+        [project(coupling, coupling_cols, mode_basis, half) for half in following], -1
+    )
+    hopping = share(coupling_part)
     energy_count = energies.shape[0]
     per_device = energy_count // lax.axis_size(("slab", "orb"))
     slot_index = lax.axis_index(("slab", "orb")) * per_device + jnp.arange(
@@ -242,7 +282,7 @@
     slot_energy = jnp.sum(
         jnp.where(positions[None, :] == selected_owner_device[:, None], energies[None, :], 0.0), 1
     )
-    green, dos = sweep(slot_energy, blocks)
+    green, dos = sweep(slot_energy, hamil, hopping)
     return (green, dos)
 
 

time: 376 us -> 314 us (0.84)
  Pallas kernels: 128 us -> 83 us
  waiting for transfers between devices: 182 us -> 163 us
  other arithmetic: 18 us -> 4.21 us
  matrix products: 14.3 us -> 24 us
  local copies, waits for them, and re-layouts: 16.5 us -> 24.1 us
    psum x1 -> x0, waiting for transfers between devices: 50.5 us -> none  [on_device(): summed = lax.psum(partial_value, 'orb')]
    pallas_call x1, Pallas kernels: 128 us -> 83 us  [sweep_one(): pl.pallas_call(sweep_kernel, out_shape=(jax.ShapeDtypeStruct((2, M, M), j...]
    reduce_scatter x0 -> x2, waiting for transfers between devices: none -> 23.6 us  [share(): own = lax.psum_scatter(rows, 'orb', scatter_dimension=1, tiled=True)]
    all_gather x3 -> x4, waiting for transfers between devices: 122 us -> 139 us  [the longest x2 82 us: share(): every = lax.all_gather(own, ('slab', 'orb'), axis=0, tiled=False)]
    all_gather x1 -> x0, other arithmetic: 14.6 us -> none  [on_device(): collected = lax.all_gather(summed, 'slab', axis=0, tiled=True)]
    dot_general x2 -> x4, matrix products: 13.2 us -> 22.4 us  [project(): jnp.einsum('scbrk,sbkm->scbrm', shaped, chosen, preferred_element_type=jn...]
    ppermute x1 -> x2, waiting for transfers between devices: 8.42 us -> 0.01 us  [shifted(): lax.ppermute(array, axis, [(i, (i + by) % size) for i in range(size)])]
    gather x6 -> x8, local copies, waits for them, and re-layouts: 10 us -> 13.8 us  [pick_blocks(): return table[index]]
  transfers between devices with their start and end apart: 5 -> 8, of which waited for: 5 -> 6; matrix products, arithmetic and copies ran while one was open for 4% -> 15% of each run, Pallas kernels for 0% -> 0%
where the time goes in v2:
time: 314 us
  waiting for transfers between devices  163 us (52%)
  Pallas kernels  83 us (26%)
  local copies, waits for them, and re-layouts  24.1 us (8%)
  matrix products  24 us (8%)
  between operations  14.3 us (5%)
  other arithmetic  4.21 us (1%)
    pallas_call x1, Pallas kernels, sweep_one(): pl.pallas_call(sweep_kernel, out_shape=(jax.ShapeDtypeStruct((2, M, M), j...  83 us
    all_gather x2, waiting for transfers between devices, share(): every = lax.all_gather(own, ('slab', 'orb'), axis=0, tiled=False)  82 us
    all_gather x2, waiting for transfers between devices, on_device(): own = [lax.all_gather(half, 'orb', axis=1, tiled=True) for half in halves]  56.8 us
    reduce_scatter x2, waiting for transfers between devices, share(): own = lax.psum_scatter(rows, 'orb', scatter_dimension=1, tiled=True)  23.6 us
    dot_general x4, matrix products, project(): jnp.einsum('scbrk,sbkm->scbrm', shaped, chosen, preferred_element_type=jn...  22.4 us
    gather x8, local copies, waits for them, and re-layouts, pick_blocks(): return table[index]  13.8 us
  transfers between devices with their start and end apart: 8, of which 6 were waited for; matrix products, arithmetic and copies ran while one was open for 15% of the time, Pallas kernels for 0%

profile of v2, /device:TPU:0, one launch (start us, length us, event | category | flops | bytes accessed | tf_op | source)
XLA Modules:
  0.0 313.6 jit_solution(17929653967443587759)
XLA Ops:
  7.2 2.0 fusion.46
  11.6 33.4 %all-gather.9.cloned.1.call-done = bf16[1,5120,128]{2,1,0:T(8,128)(2,1)} async-done(((bf16[1,1280,128]{2,1,0:T(8,128)(2,1)}), bf16[1,5120,128]{2,1,0:T(8,128)(2,1)}) %all-gather.9.cloned.1.call-update) | async-done | bytes 1310736 | tf_op jit(solution)/shard_map/all_gather | solution.py:261
  45.0 3.8 %gather_fusion.1 = bf16[64,160,128]{2,1,0:T(8,128)(2,1)} fusion(bf16[1,32,160,128]{3,2,1,0:T(8,128)(2,1)} %bitcast.101, s32[64]{0:T(128)S(1)} %reshape.130), kind=kCustom, calls=%fused_computation.1 | custom fusion | bytes 5243392 | tf_op jit(solution)/shard_map/vmap()/gather | solution.py:225
  49.1 6.4 %fusion.26 = bf16[1,2,8,160,128]{4,3,1,2,0:T(8,128)(2,1)} fusion(bf16[8,1280,128,1]{2,1,3,0:T(8,128)(2,1)} %bitcast.104, bf16[2,8,160,1280]{3,2,1,0:T(8,128)(2,1)} %bitcast.113), kind=kOutput, calls=%fused_computation.18 | convolution fusion | flops 839188480 | bytes 9830400 | tf_op jit(solution)/shard_map/scbrk,sbkm->scbrm/dot_general | solution.py:236
  55.5 23.4 %all-gather.7.cloned.1.call-done = bf16[1,5120,128]{2,1,0:T(8,128)(2,1)} async-done(((bf16[1,1280,128]{2,1,0:T(8,128)(2,1)}), bf16[1,5120,128]{2,1,0:T(8,128)(2,1)}) %all-gather.7.cloned.1.call-update) | async-done | bytes 1310736 | tf_op jit(solution)/shard_map/all_gather | solution.py:261
  78.9 3.8 %gather_fusion = bf16[64,160,128]{2,1,0:T(8,128)(2,1)} fusion(bf16[1,32,160,128]{3,2,1,0:T(8,128)(2,1)} %bitcast.102, s32[64]{0:T(128)S(1)} %reshape.130), kind=kCustom, calls=%fused_computation | custom fusion | bytes 5243392 | tf_op jit(solution)/shard_map/vmap()/gather | solution.py:225
  82.9 5.6 %fusion.29 = bf16[1,2,8,160,128]{4,3,1,2,0:T(8,128)(2,1)S(1)} fusion(bf16[8,1280,128,1]{2,1,3,0:T(8,128)(2,1)} %bitcast.103, bf16[2,8,160,1280]{3,2,1,0:T(8,128)(2,1)} %bitcast.114), kind=kOutput, calls=%fused_computation.19 | convolution fusion | flops 839188480 | bytes 9830400 | tf_op jit(solution)/shard_map/scbrk,sbkm->scbrm/dot_general | solution.py:236
  88.6 1.0 copy-done.2
  90.4 0.8 pad_maximum_fusion
  91.2 2.1 copy.33
  93.4 3.7 %gather_fusion.3 = bf16[64,160,128]{2,1,0:T(8,128)(2,1)} fusion(bf16[1,32,160,128]{3,2,1,0:T(8,128)(2,1)} %bitcast.38, s32[64]{0:T(128)S(1)} %reshape.146), kind=kCustom, calls=%fused_computation.3 | custom fusion | bytes 5243392 | tf_op jit(solution)/shard_map/vmap()/gather | solution.py:225
  97.1 5.6 %fusion.20 = bf16[1,2,8,160,128]{4,3,1,2,0:T(8,128)(2,1)S(1)} fusion(bf16[8,1280,128,1]{2,1,3,0:T(8,128)(2,1)} %bitcast.106, bf16[2,8,160,1280]{3,2,1,0:T(8,128)(2,1)} %bitcast.115), kind=kOutput, calls=%fused_computation.16 | convolution fusion | flops 839188480 | bytes 9830400 | tf_op jit(solution)/shard_map/scbrk,sbkm->scbrm/dot_general | solution.py:236
  102.7 0.9 copy.38
  103.6 2.4 gather_fusion.2
  106.0 4.9 %fusion.23 = bf16[1,2,8,160,128]{4,3,1,2,0:T(8,128)(2,1)S(1)} fusion(bf16[8,1280,128,1]{2,1,3,0:T(8,128)(2,1)S(1)} %bitcast.105, bf16[2,8,160,1280]{3,2,1,0:T(8,128)(2,1)} %bitcast.116), kind=kOutput, calls=%fused_computation.17 | convolution fusion | flops 839188480 | bytes 9830400 | tf_op jit(solution)/shard_map/scbrk,sbkm->scbrm/dot_general | solution.py:236
  111.7 1.0 copy.40
  112.8 1.2 reduce-scatter.3.cloned.1.call-done
  114.3 22.4 %reduce-scatter.5.cloned.1.call-done = f32[1,128,256]{2,1,0:T(8,128)} async-done(((f32[1,512,256]{2,1,0:T(8,128)}), f32[1,128,256]{2,1,0:T(8,128)}) %reduce-scatter.5.cloned.1.call-update) | async-done | bytes 131088 | tf_op jit(solution)/shard_map/reduce_scatter | solution.py:253
  137.3 1.3 fusion.45
  138.6 39.8 %all-gather.11.cloned.1.call-done = f32[16,128,256]{2,1,0:T(8,128)} async-done(((f32[1,128,256]{2,1,0:T(8,128)}), f32[16,128,256]{2,1,0:T(8,128)}) %all-gather.11.cloned.1.call-update) | async-done | bytes 2097168 | tf_op jit(solution)/shard_map/all_gather | solution.py:254
  178.4 42.2 %all-gather.13.cloned.1.call-done = f32[16,128,256]{2,1,0:T(8,128)} async-done(((f32[1,128,256]{2,1,0:T(8,128)}), f32[16,128,256]{2,1,0:T(8,128)}) %all-gather.13.cloned.1.call-update) | async-done | bytes 2097168 | tf_op jit(solution)/shard_map/all_gather | solution.py:254
  220.6 1.6 copy-done
  222.2 1.6 copy-done.1
  223.8 83.0 %shard_map.86 = (f32[2,256,256]{2,1,0:T(8,128)}, f32[4]{0:T(128)}) custom-call(f32[1]{0:T(128)} %bitcast.energy_ref, f32[4,2,256,256]{3,2,1,0:T(8,128)S(1)} %bitcast.99, f32[4,2,256,256]{3,2,1,0:T(8,128)S(1)} %bitcast.100), custom_call_target="tpu_custom_call" | custom-call | tf_op jit(solution)/shard_map/pallas_call | solution.py:198
  (48 shorter events, 5.6 us)
Async XLA Ops:
  7.2 37.8 %all-gather.9.cloned.1.call-start = ((), (), s32[]{:S(2)}) async-start(), calls=%async_computation.3 | async-start | bytes 1638400 | tf_op jit(solution)/shard_map/all_gather | solution.py:261
  9.2 69.7 %all-gather.7.cloned.1.call-start = ((), (), s32[]{:S(2)}) async-start(), calls=%async_computation.2 | async-start | bytes 1638400 | tf_op jit(solution)/shard_map/all_gather | solution.py:261
  9.9 104.1 %reduce-scatter.3.cloned.1.call-start = ((), (), s32[]{:S(2)}) async-start(), calls=%async_computation.4 | async-start | bytes 655360 | tf_op jit(solution)/shard_map/reduce_scatter | solution.py:253
  45.0 3.8 %copy-start.3 = (bf16[1,5120,128]{2,1,0:T(8,128)(2,1)S(1)}, bf16[1,5120,128]{2,1,0:T(8,128)(2,1)}, u32[]{:S(2)}) copy-start(bf16[1,5120,128]{2,1,0:T(8,128)(2,1)} %all-gather.9.cloned.1.call-done) | copy-start | bytes 3932164
  48.8 44.5 %collective-permute-start.1 = (bf16[1,5120,128]{2,1,0:T(8,128)(2,1)S(1)}, bf16[1,5120,128]{2,1,0:T(8,128)(2,1)}, u32[]{:S(2)}, u32[]{:S(2)}) collective-permute-start(bf16[1,5120,128]{2,1,0:T(8,128)(2,1)S(1)} %copy-done.3), channel_id=1, source_target_pairs={{0,12},{4,0},{8,4},{12,8},{1,13},{5,1},{9,5},{13,9},{2,14},{6,2},{... | collective-permute-start | bytes 3932168 | tf_op jit(solution)/shard_map/ppermute | solution.py:20
  78.9 3.8 %copy-start.4 = (bf16[1,5120,128]{2,1,0:T(8,128)(2,1)S(1)}, bf16[1,5120,128]{2,1,0:T(8,128)(2,1)}, u32[]{:S(2)}) copy-start(bf16[1,5120,128]{2,1,0:T(8,128)(2,1)} %all-gather.7.cloned.1.call-done) | copy-start | bytes 3932164
  82.7 20.9 %collective-permute-start = (bf16[1,5120,128]{2,1,0:T(8,128)(2,1)S(1)}, bf16[1,5120,128]{2,1,0:T(8,128)(2,1)}, u32[]{:S(2)}, u32[]{:S(2)}) collective-permute-start(bf16[1,5120,128]{2,1,0:T(8,128)(2,1)S(1)} %copy-done.4), channel_id=1, source_target_pairs={{0,12},{4,0},{8,4},{12,8},{1,13},{5,1},{9,5},{13,9},{2,14},{6,2},{... | collective-permute-start | bytes 3932168 | tf_op jit(solution)/shard_map/ppermute | solution.py:20
  82.9 5.6 %copy-start.6 = (bf16[1,2,8,160,128]{4,3,1,2,0:T(8,128)(2,1)S(1)}, bf16[1,2,8,160,128]{4,3,1,2,0:T(8,128)(2,1)}, u32[]{:S(2)}) copy-start(bf16[1,2,8,160,128]{4,3,1,2,0:T(8,128)(2,1)} %fusion.26) | copy-start | bytes 1966084
  88.5 1.1 copy-start.2
  93.3 43.4 %reduce-scatter.5.cloned.1.call-start = ((), (), s32[]{:S(2)}) async-start(), calls=%async_computation.5 | async-start | bytes 655360 | tf_op jit(solution)/shard_map/reduce_scatter | solution.py:253
  106.0 4.9 %copy-start.5 = (bf16[1,2,8,160,128]{4,3,2,1,0:T(8,128)(2,1)S(1)}, bf16[1,2,8,160,128]{4,3,2,1,0:T(8,128)(2,1)}, u32[]{:S(2)}) copy-start(bf16[1,2,8,160,128]{4,3,2,1,0:T(8,128)(2,1)} %copy.38) | copy-start | bytes 1966084
  111.3 25.4 %copy-start.7 = (s32[16]{0:T(128)S(1)}, s32[16]{0:T(128)}, u32[]{:S(2)}) copy-start(s32[16]{0:T(128)} %param.13) | copy-start | bytes 196
  111.3 26.0 %copy-start.8 = (f32[16]{0:T(128)S(1)}, f32[16]{0:T(128)}, u32[]{:S(2)}) copy-start(f32[16]{0:T(128)} %param.12) | copy-start | bytes 196
  112.8 65.7 %all-gather.11.cloned.1.call-start = ((), (), s32[]{:S(2)}) async-start(), calls=%async_computation.6 | async-start | bytes 2228224 | tf_op jit(solution)/shard_map/all_gather | solution.py:254
  114.0 106.6 %all-gather.13.cloned.1.call-start = ((), (), s32[]{:S(2)}) async-start(), calls=%async_computation.7 | async-start | bytes 2228224 | tf_op jit(solution)/shard_map/all_gather | solution.py:254
  220.6 1.6 copy-start
  222.2 1.6 copy-start.1
Sparse Core Ops, SparseCore 0:
  9.6 35.3 all-gather.8
  47.1 31.6 all-gather.6
  93.4 20.5 reduce-scatter.2
  116.7 19.9 reduce-scatter.4
  138.7 39.6 all-gather.10
  180.5 40.0 all-gather.12

commit v3 on v2

--- a/solution.py
+++ b/solution.py
@@ -130,7 +130,7 @@
     return value[0].T, -value[1].T
 
 
-def sweep_kernel(energy_ref, hamil_ref, hopping_ref, green_ref, dos_ref, work_re, work_im):
+def sweep_kernel(energy_ref, places_ref, hamil_ref, hopping_ref, green_ref, dos_ref, work_re, work_im):
     eye = lax.broadcasted_iota(jnp.int32, (M, M), 0) == lax.broadcasted_iota(jnp.int32, (M, M), 1)
     energy = energy_ref[0]
 
@@ -151,7 +151,8 @@
 
     def step(s, _):
         lead = s == 0
-        hop = jnp.where(lead, hamil_ref.shape[0] - 1, s - 1)
+        hop = places_ref[jnp.where(lead, hamil_ref.shape[0] - 1, s - 1)]
+        here = places_ref[s]
         t = (hopping_ref[hop, 0], hopping_ref[hop, 1])
         t_adj = adjoint(t)
 
@@ -167,7 +168,7 @@
             green_ref[0] = self_energy[0]
             green_ref[1] = self_energy[1]
 
-        raw_re, raw_im = hamil_ref[s, 0], hamil_ref[s, 1]
+        raw_re, raw_im = hamil_ref[here, 0], hamil_ref[here, 1]
         ham_re = (raw_re + raw_re.T) / 2.0
         ham_im = (raw_im - raw_im.T) / 2.0
         green_ref[0] = jnp.where(eye, energy, 0.0) - ham_re - green_ref[0]
@@ -194,7 +195,7 @@
     lax.fori_loop(0, hamil_ref.shape[0], step, 0)
 
 
-def sweep_one(energy, hamil, hopping):
+def sweep_one(energy, places, hamil, hopping):
     green, dos = pl.pallas_call(
         sweep_kernel,
         out_shape=(
@@ -202,6 +203,7 @@
             jax.ShapeDtypeStruct((hamil.shape[0],), jnp.float32),
         ),
         in_specs=[
+            pl.BlockSpec(memory_space=pltpu.SMEM),
             pl.BlockSpec(memory_space=pltpu.SMEM),
             pl.BlockSpec(memory_space=pltpu.VMEM),
             pl.BlockSpec(memory_space=pltpu.VMEM),
@@ -212,12 +214,12 @@
         ),
         scratch_shapes=[pltpu.VMEM((TILES, 8, HALF), jnp.float32)] * 2,
         compiler_params=pltpu.CompilerParams(vmem_limit_bytes=40 * 1024 * 1024),
-    )(energy.reshape(1), hamil, hopping)
+    )(energy.reshape(1), places, hamil, hopping)
     return green, dos
 
 
-def sweep(energy, hamil, hopping):
-    pairs = [sweep_one(energy[e], hamil, hopping) for e in range(energy.shape[0])]
+def sweep(energy, places, hamil, hopping):
+    pairs = [sweep_one(energy[e], places, hamil, hopping) for e in range(energy.shape[0])]
     return jnp.stack([p[0] for p in pairs]), jnp.stack([p[1] for p in pairs])
 
 
@@ -249,11 +251,48 @@
 
 def share(partial_value):
     slab_count = partial_value.shape[0]
-    rows = partial_value.reshape(slab_count, 2 * M, M)
-    own = lax.psum_scatter(rows, "orb", scatter_dimension=1, tiled=True)
-    every = lax.all_gather(own, ("slab", "orb"), axis=0, tiled=False)
-    every = every.reshape(lax.axis_size("slab"), lax.axis_size("orb"), slab_count, -1, M)
-    return jnp.swapaxes(every, 1, 2).reshape(-1, 2, M, M)
+    size = lax.axis_size("orb")
+    if size <= 8:
+        me = lax.axis_index("orb")
+        pieces = partial_value.reshape(slab_count, size, 2 * M // size, M)
+
+        def piece(which):
+            return lax.dynamic_index_in_dim(pieces, lax.rem(which, size), 1, keepdims=True)
+
+        own = piece(me)
+        for by in [shifted(piece(me + k), "orb", k) for k in range(1, size)]:
+            own = own + by
+        moved = [own] + [shifted(own, "orb", k) for k in range(1, size)]
+        summed = jnp.zeros_like(pieces)
+        for k in range(size):
+            place = lax.rem(me + size - k, size)
+            summed = lax.dynamic_update_slice_in_dim(summed, moved[k], place, 1)
+    else:
+        summed = lax.psum(partial_value, "orb")
+    blocks = summed.reshape(slab_count, 2, M, M)
+    slabs = lax.axis_size("slab")
+    if slabs & (slabs - 1):
+        return lax.all_gather(blocks, "slab", axis=0, tiled=True)
+    bit = slabs // 2
+    while bit:
+        other = lax.ppermute(blocks, "slab", [(i, i ^ bit) for i in range(slabs)])
+        blocks = jnp.concatenate([blocks, other], 0)
+        bit //= 2
+    return blocks
+
+
+def slab_places(slab_count):
+    slabs = lax.axis_size("slab")
+    device = jnp.arange(slabs, dtype=jnp.int32)
+    if slabs & (slabs - 1) == 0:
+        apart = device ^ lax.axis_index("slab")
+        device = jnp.zeros_like(apart)
+        bit, weight = slabs // 2, 1
+        while bit:
+            device = device + jnp.where((apart & bit) != 0, weight, 0)
+            bit, weight = bit // 2, weight * 2
+    inside = jnp.arange(slab_count, dtype=jnp.int32)
+    return (device[:, None] * slab_count + inside[None, :]).reshape(-1)
 
 
 def on_device(mode_basis, onsite, onsite_cols, coupling, coupling_cols, energies, owner):
@@ -270,6 +309,7 @@
         [project(coupling, coupling_cols, mode_basis, half) for half in following], -1
     )
     hopping = share(coupling_part)
+    places = slab_places(mode_basis.shape[0])
     energy_count = energies.shape[0]
     per_device = energy_count // lax.axis_size(("slab", "orb"))
     slot_index = lax.axis_index(("slab", "orb")) * per_device + jnp.arange(
@@ -282,7 +322,7 @@
     slot_energy = jnp.sum(
         jnp.where(positions[None, :] == selected_owner_device[:, None], energies[None, :], 0.0), 1
     )
-    green, dos = sweep(slot_energy, hamil, hopping)
+    green, dos = sweep(slot_energy, places, hamil, hopping)
     return (green, dos)
 
 

time: 314 us -> 286 us (0.911); the launches traced: 314 us -> 281 us
  waiting for transfers between devices: 163 us -> 104 us
  starting transfers between devices: 0.92 us -> 25.7 us
  other arithmetic: 4.21 us -> 9.19 us
    all_gather x2 -> x0, waiting for transfers between devices: 82 us -> none  [share(): every = lax.all_gather(own, ('slab', 'orb'), axis=0, tiled=False)]
    ppermute x2 -> x14, waiting for transfers between devices: 0.01 us -> 26 us  [shifted(): lax.ppermute(array, axis, [(i, (i + by) % size) for i in range(size)])]
    ppermute x2 -> x14, starting transfers between devices: 0.5 us -> 24.7 us  [shifted(): lax.ppermute(array, axis, [(i, (i + by) % size) for i in range(size)])]
    reduce_scatter x2 -> x0, waiting for transfers between devices: 23.6 us -> none  [share(): own = lax.psum_scatter(rows, 'orb', scatter_dimension=1, tiled=True)]
    ppermute x0 -> x4, waiting for transfers between devices: none -> 13.3 us  [share(): other = lax.ppermute(blocks, 'slab', [(i, i ^ bit) for i in range(slabs)])]
    all_gather x2, waiting for transfers between devices: 56.8 us -> 64.3 us  [on_device(): own = [lax.all_gather(half, 'orb', axis=1, tiled=True) for half in halves]]
    concatenate x0 -> x4, other arithmetic: none -> 3.94 us  [share(): blocks = jnp.concatenate([blocks, other], 0)]
    unnamed x18 -> x16, local copies, waits for them, and re-layouts: 4.19 us -> 1.01 us
  transfers between devices with their start and end apart: 8 -> 20, of which waited for: 6 -> 11; matrix products, arithmetic and copies ran while one was open for 15% -> 14% of each run, Pallas kernels for 0% -> 0%
where the time goes in v3:
time: 286 us; the launch traced here: 281 us
  waiting for transfers between devices  104 us (36%)
  Pallas kernels  83.6 us (29%)
  starting transfers between devices  25.7 us (9%)
  matrix products  22.1 us (8%)
  local copies, waits for them, and re-layouts  21.9 us (8%)
  between operations  14.4 us (5%)
  other arithmetic  9.19 us (3%)
    pallas_call x1, Pallas kernels, sweep_one(): pl.pallas_call(sweep_kernel, out_shape=(jax.ShapeDtypeStruct((2, M, M), j...  83.6 us
    all_gather x2, waiting for transfers between devices, on_device(): own = [lax.all_gather(half, 'orb', axis=1, tiled=True) for half in halves]  64.3 us
    ppermute x14, waiting for transfers between devices, shifted(): lax.ppermute(array, axis, [(i, (i + by) % size) for i in range(size)])  26 us
    ppermute x14, starting transfers between devices, shifted(): lax.ppermute(array, axis, [(i, (i + by) % size) for i in range(size)])  24.7 us
    dot_general x4, matrix products, project(): jnp.einsum('scbrk,sbkm->scbrm', shaped, chosen, preferred_element_type=jn...  20.6 us
    gather x8, local copies, waits for them, and re-layouts, pick_blocks(): return table[index]  13.7 us
    ppermute x4, waiting for transfers between devices, share(): other = lax.ppermute(blocks, 'slab', [(i, i ^ bit) for i in range(slabs)])  13.3 us
  transfers between devices with their start and end apart: 20, of which 11 were waited for; matrix products, arithmetic and copies ran while one was open for 14% of the time, Pallas kernels for 0%

profile of v3, /device:TPU:0, one launch (start us, length us, event | category | flops | bytes accessed | tf_op | source)
XLA Modules:
  0.0 281.2 jit_solution(13975700913061737003)
XLA Ops:
  7.2 1.9 fusion.47
  10.8 34.2 %all-gather.5.cloned.1.call-done = bf16[1,5120,128]{2,1,0:T(8,128)(2,1)} async-done(((bf16[1,1280,128]{2,1,0:T(8,128)(2,1)}), bf16[1,5120,128]{2,1,0:T(8,128)(2,1)}) %all-gather.5.cloned.1.call-update) | async-done | bytes 1310736 | tf_op jit(solution)/shard_map/all_gather | solution.py:300
  45.0 3.7 %gather_fusion.1 = bf16[64,160,128]{2,1,0:T(8,128)(2,1)} fusion(bf16[1,32,160,128]{3,2,1,0:T(8,128)(2,1)} %bitcast.100, s32[64]{0:T(128)S(1)} %reshape.138), kind=kCustom, calls=%fused_computation.1 | custom fusion | bytes 5243392 | tf_op jit(solution)/shard_map/vmap()/gather | solution.py:227
  48.7 30.1 %all-gather.3.cloned.1.call-done = bf16[1,5120,128]{2,1,0:T(8,128)(2,1)} async-done(((bf16[1,1280,128]{2,1,0:T(8,128)(2,1)}), bf16[1,5120,128]{2,1,0:T(8,128)(2,1)}) %all-gather.3.cloned.1.call-update) | async-done | bytes 1310736 | tf_op jit(solution)/shard_map/all_gather | solution.py:300
  78.9 3.7 %gather_fusion = bf16[64,160,128]{2,1,0:T(8,128)(2,1)} fusion(bf16[1,32,160,128]{3,2,1,0:T(8,128)(2,1)} %bitcast.99, s32[64]{0:T(128)S(1)} %reshape.138), kind=kCustom, calls=%fused_computation | custom fusion | bytes 5243392 | tf_op jit(solution)/shard_map/vmap()/gather | solution.py:227
  82.6 5.6 %fusion.26 = bf16[1,2,8,160,128]{4,3,1,2,0:T(8,128)(2,1)S(1)} fusion(bf16[8,1280,128,1]{2,1,3,0:T(8,128)(2,1)} %bitcast.108, bf16[2,8,160,1280]{3,2,1,0:T(8,128)(2,1)} %bitcast.119), kind=kOutput, calls=%fused_computation.20 | convolution fusion | flops 839188480 | bytes 9830400 | tf_op jit(solution)/shard_map/scbrk,sbkm->scbrm/dot_general | solution.py:238
  88.5 4.7 %fusion.29 = bf16[1,2,8,160,128]{4,3,1,2,0:T(8,128)(2,1)S(1)} fusion(bf16[8,1280,128,1]{2,1,3,0:T(8,128)(2,1)S(1)} %bitcast.107, bf16[2,8,160,1280]{3,2,1,0:T(8,128)(2,1)} %bitcast.120), kind=kOutput, calls=%fused_computation.21 | convolution fusion | flops 839188480 | bytes 9830400 | tf_op jit(solution)/shard_map/scbrk,sbkm->scbrm/dot_general | solution.py:238
  96.0 2.0 copy.19
  103.1 2.4 collective-permute-start.2
  105.5 4.1 %collective-permute-done = f32[1,1,128,256]{3,2,1,0:T(8,128)S(1)} collective-permute-done((f32[1,1,128,256]{3,2,1,0:T(8,128)}, f32[1,1,128,256]{3,2,1,0:T(8,128)S(1)}, u32[]{:S(2)}, u32[]{:S(2)}) %collective-permute-start) | collective-permute-done | bytes 131104 | tf_op jit(solution)/shard_map/ppermute | solution.py:20
  109.6 3.8 %collective-permute-done.1 = f32[1,1,128,256]{3,2,1,0:T(8,128)S(1)} collective-permute-done((f32[1,1,128,256]{3,2,1,0:T(8,128)}, f32[1,1,128,256]{3,2,1,0:T(8,128)S(1)}, u32[]{:S(2)}, u32[]{:S(2)}) %collective-permute-start.1) | collective-permute-done | bytes 131104 | tf_op jit(solution)/shard_map/ppermute | solution.py:20
  115.1 3.4 %collective-permute-start.3 = (f32[1,1,128,256]{3,2,1,0:T(8,128)}, f32[1,1,128,256]{3,2,1,0:T(8,128)}, u32[]{:S(2)}, u32[]{:S(2)}) collective-permute-start(f32[1,1,128,256]{3,2,1,0:T(8,128)} %get-tuple-element.9), channel_id=1, source_target_pairs={{0,1},{1,2},{2,3},{3,0},{4,5},{5,6},{6,7},{7,4},{8,9},{9,10},{10,1... | collective-permute-start | bytes 393224 | tf_op jit(solution)/shard_map/ppermute | solution.py:20
  118.5 3.7 %gather_fusion.3 = bf16[64,160,128]{2,1,0:T(8,128)(2,1)} fusion(bf16[1,32,160,128]{3,2,1,0:T(8,128)(2,1)} %bitcast.38, s32[64]{0:T(128)S(1)} %reshape.154), kind=kCustom, calls=%fused_computation.3 | custom fusion | bytes 5243392 | tf_op jit(solution)/shard_map/vmap()/gather | solution.py:227
  122.2 5.5 %fusion.20 = bf16[1,2,8,160,128]{4,3,1,2,0:T(8,128)(2,1)S(1)} fusion(bf16[8,1280,128,1]{2,1,3,0:T(8,128)(2,1)} %bitcast.110, bf16[2,8,160,1280]{3,2,1,0:T(8,128)(2,1)} %bitcast.121), kind=kOutput, calls=%fused_computation.18 | convolution fusion | flops 839188480 | bytes 9830400 | tf_op jit(solution)/shard_map/scbrk,sbkm->scbrm/dot_general | solution.py:238
  128.2 2.4 gather_fusion.2
  130.5 4.8 %fusion.23 = bf16[1,2,8,160,128]{4,3,1,2,0:T(8,128)(2,1)S(1)} fusion(bf16[8,1280,128,1]{2,1,3,0:T(8,128)(2,1)S(1)} %bitcast.109, bf16[2,8,160,1280]{3,2,1,0:T(8,128)(2,1)} %bitcast.122), kind=kOutput, calls=%fused_computation.19 | convolution fusion | flops 839188480 | bytes 9830400 | tf_op jit(solution)/shard_map/scbrk,sbkm->scbrm/dot_general | solution.py:238
  137.9 2.1 collective-permute-start.12
  144.3 6.0 %collective-permute-done.11 = f32[1,1,128,256]{3,2,1,0:T(8,128)S(1)} collective-permute-done((f32[1,1,128,256]{3,2,1,0:T(8,128)S(1)}, f32[1,1,128,256]{3,2,1,0:T(8,128)S(1)}, u32[]{:S(2)}, u32[]{:S(2)}) %collective-permute-start.11) | collective-permute-done | bytes 131104 | tf_op jit(solution)/shard_map/ppermute | solution.py:20
  150.5 4.9 %collective-permute-start.13 = (f32[1,1,128,256]{3,2,1,0:T(8,128)S(1)}, f32[1,1,128,256]{3,2,1,0:T(8,128)S(1)}, u32[]{:S(2)}, u32[]{:S(2)}) collective-permute-start(f32[1,1,128,256]{3,2,1,0:T(8,128)S(1)} %get-tuple-element.7), channel_id=1, source_target_pairs={{0,1},{1,2},{2,3},{3,0},{4,5},{5,6},{6,7},{7,4},{8,9},{9,10},{10,1... | collective-permute-start | bytes 393224 | tf_op jit(solution)/shard_map/ppermute | solution.py:20
  159.3 1.9 collective-permute-start.15
  162.4 5.9 %collective-permute-done.14 = f32[1,1,128,256]{3,2,1,0:T(8,128)S(1)} collective-permute-done((f32[1,1,128,256]{3,2,1,0:T(8,128)S(1)}, f32[1,1,128,256]{3,2,1,0:T(8,128)S(1)}, u32[]{:S(2)}, u32[]{:S(2)}) %collective-permute-start.14) | collective-permute-done | bytes 131104 | tf_op jit(solution)/shard_map/ppermute | solution.py:20
  168.3 2.7 collective-permute-done.15
  171.6 13.3 %collective-permute-done.16 = f32[1,2,256,256]{3,2,1,0:T(8,128)S(1)} collective-permute-done((f32[1,2,256,256]{3,2,1,0:T(8,128)S(1)}, f32[1,2,256,256]{3,2,1,0:T(8,128)S(1)}, u32[]{:S(2)}, u32[]{:S(2)}) %collective-permute-start.16) | collective-permute-done | bytes 524320 | tf_op jit(solution)/shard_map/ppermute | solution.py:278
  190.8 83.6 %shard_map.86 = (f32[2,256,256]{2,1,0:T(8,128)}, f32[4]{0:T(128)}) custom-call(f32[1]{0:T(128)} %bitcast.energy_ref, s32[4]{0:T(128)S(1)} %fusion.46.places_ref, f32[4,2,256,256]{3,2,1,0:T(8,128)S(1)} %pad_maximum_fusion.hamil_ref, f32[4,2,256,256]{3,2,1,0:T(8,128)S(1)} %pad_maximum_fusion.1.hopping_ref), custom_call_target="tpu_custom_call" | custom-call | tf_op jit(solution)/shard_map/pallas_call | solution.py:199
  (82 shorter events, 30.2 us)
Async XLA Ops:
  7.2 37.8 %all-gather.5.cloned.1.call-start = ((), (), s32[]{:S(2)}) async-start(), calls=%async_computation.1 | async-start | bytes 1638400 | tf_op jit(solution)/shard_map/all_gather | solution.py:300
  9.2 69.7 %all-gather.3.cloned.1.call-start = ((), (), s32[]{:S(2)}) async-start(), calls=%async_computation | async-start | bytes 1638400 | tf_op jit(solution)/shard_map/all_gather | solution.py:300
  82.6 6.0 %copy-start.5 = (bf16[64,160,128]{2,1,0:T(8,128)(2,1)S(1)}, bf16[64,160,128]{2,1,0:T(8,128)(2,1)}, u32[]{:S(2)}) copy-start(bf16[64,160,128]{2,1,0:T(8,128)(2,1)} %gather_fusion) | copy-start | bytes 7864324
  88.2 30.3 %collective-permute-start.9 = (bf16[1,5120,128]{2,1,0:T(8,128)(2,1)S(1)}, bf16[1,5120,128]{2,1,0:T(8,128)(2,1)}, u32[]{:S(2)}, u32[]{:S(2)}) collective-permute-start(bf16[1,5120,128]{2,1,0:T(8,128)(2,1)S(1)} %copy-done.2), channel_id=1, source_target_pairs={{0,12},{4,0},{8,4},{12,8},{1,13},{5,1},{9,5},{13,9},{2,14},{6,2},{... | collective-permute-start | bytes 3932168 | tf_op jit(solution)/shard_map/ppermute | solution.py:20
  98.0 30.2 %collective-permute-start.8 = (bf16[1,5120,128]{2,1,0:T(8,128)(2,1)S(1)}, bf16[1,5120,128]{2,1,0:T(8,128)(2,1)}, u32[]{:S(2)}, u32[]{:S(2)}) collective-permute-start(bf16[1,5120,128]{2,1,0:T(8,128)(2,1)S(1)} %copy-done.1), channel_id=1, source_target_pairs={{0,12},{4,0},{8,4},{12,8},{1,13},{5,1},{9,5},{13,9},{2,14},{6,2},{... | collective-permute-start | bytes 3932168 | tf_op jit(solution)/shard_map/ppermute | solution.py:20
  101.1 8.5 %collective-permute-start = (f32[1,1,128,256]{3,2,1,0:T(8,128)}, f32[1,1,128,256]{3,2,1,0:T(8,128)S(1)}, u32[]{:S(2)}, u32[]{:S(2)}) collective-permute-start(f32[1,1,128,256]{3,2,1,0:T(8,128)} %get-tuple-element.15), channel_id=1, source_target_pairs={{0,1},{1,2},{2,3},{3,0},{4,5},{5,6},{6,7},{7,4},{8,9},{9,10},{10,1... | collective-permute-start | bytes 393224 | tf_op jit(solution)/shard_map/ppermute | solution.py:20
  101.9 11.5 %collective-permute-start.1 = (f32[1,1,128,256]{3,2,1,0:T(8,128)}, f32[1,1,128,256]{3,2,1,0:T(8,128)S(1)}, u32[]{:S(2)}, u32[]{:S(2)}) collective-permute-start(f32[1,1,128,256]{3,2,1,0:T(8,128)} %get-tuple-element.17), channel_id=1, source_target_pairs={{0,2},{1,3},{2,0},{3,1},{4,6},{5,7},{6,4},{7,5},{8,10},{9,11},{10,... | collective-permute-start | bytes 393224 | tf_op jit(solution)/shard_map/ppermute | solution.py:20
  103.1 10.3 %collective-permute-start.2 = (f32[1,1,128,256]{3,2,1,0:T(8,128)}, f32[1,1,128,256]{3,2,1,0:T(8,128)}, u32[]{:S(2)}, u32[]{:S(2)}) collective-permute-start(f32[1,1,128,256]{3,2,1,0:T(8,128)} %get-tuple-element.16), channel_id=1, source_target_pairs={{0,3},{1,0},{2,1},{3,2},{4,7},{5,4},{6,5},{7,6},{8,11},{9,8},{10,9... | collective-permute-start | bytes 393224 | tf_op jit(solution)/shard_map/ppermute | solution.py:20
  115.1 26.8 %collective-permute-start.3 = (f32[1,1,128,256]{3,2,1,0:T(8,128)}, f32[1,1,128,256]{3,2,1,0:T(8,128)}, u32[]{:S(2)}, u32[]{:S(2)}) collective-permute-start(f32[1,1,128,256]{3,2,1,0:T(8,128)} %get-tuple-element.9), channel_id=1, source_target_pairs={{0,1},{1,2},{2,3},{3,0},{4,5},{5,6},{6,7},{7,4},{8,9},{9,10},{10,1... | collective-permute-start | bytes 393224 | tf_op jit(solution)/shard_map/ppermute | solution.py:20
  135.3 7.5 %copy-start.4 = (f32[1,4,128,256]{3,2,1,0:T(8,128)S(1)}, f32[1,4,128,256]{3,2,1,0:T(8,128)}, u32[]{:S(2)}) copy-start(f32[1,4,128,256]{3,2,1,0:T(8,128)} %copy-done.3) | copy-start | bytes 1572868
  136.0 8.3 %collective-permute-start.10 = (f32[1,1,128,256]{3,2,1,0:T(8,128)S(1)}, f32[1,1,128,256]{3,2,1,0:T(8,128)S(1)}, u32[]{:S(2)}, u32[]{:S(2)}) collective-permute-start(f32[1,1,128,256]{3,2,1,0:T(8,128)S(1)} %get-tuple-element.12), channel_id=1, source_target_pairs={{0,1},{1,2},{2,3},{3,0},{4,5},{5,6},{6,7},{7,4},{8,9},{9,10},{10,1... | collective-permute-start | bytes 393224 | tf_op jit(solution)/shard_map/ppermute | solution.py:20
  136.9 13.5 %collective-permute-start.11 = (f32[1,1,128,256]{3,2,1,0:T(8,128)S(1)}, f32[1,1,128,256]{3,2,1,0:T(8,128)S(1)}, u32[]{:S(2)}, u32[]{:S(2)}) collective-permute-start(f32[1,1,128,256]{3,2,1,0:T(8,128)S(1)} %get-tuple-element.14), channel_id=1, source_target_pairs={{0,2},{1,3},{2,0},{3,1},{4,6},{5,7},{6,4},{7,5},{8,10},{9,11},{10,... | collective-permute-start | bytes 393224 | tf_op jit(solution)/shard_map/ppermute | solution.py:20
  137.9 12.4 %collective-permute-start.12 = (f32[1,1,128,256]{3,2,1,0:T(8,128)S(1)}, f32[1,1,128,256]{3,2,1,0:T(8,128)S(1)}, u32[]{:S(2)}, u32[]{:S(2)}) collective-permute-start(f32[1,1,128,256]{3,2,1,0:T(8,128)S(1)} %get-tuple-element.13), channel_id=1, source_target_pairs={{0,3},{1,0},{2,1},{3,2},{4,7},{5,4},{6,5},{7,6},{8,11},{9,8},{10,9... | collective-permute-start | bytes 393224 | tf_op jit(solution)/shard_map/ppermute | solution.py:20
  140.1 17.1 %collective-permute-start.4 = (f32[1,1,128,256]{3,2,1,0:T(8,128)}, f32[1,1,128,256]{3,2,1,0:T(8,128)S(1)}, u32[]{:S(2)}, u32[]{:S(2)}) collective-permute-start(f32[1,1,128,256]{3,2,1,0:T(8,128)} %get-tuple-element.9), channel_id=1, source_target_pairs={{0,2},{1,3},{2,0},{3,1},{4,6},{5,7},{6,4},{7,5},{8,10},{9,11},{10,... | collective-permute-start | bytes 393224 | tf_op jit(solution)/shard_map/ppermute | solution.py:20
  141.9 16.9 %collective-permute-start.5 = (f32[1,1,128,256]{3,2,1,0:T(8,128)}, f32[1,1,128,256]{3,2,1,0:T(8,128)S(1)}, u32[]{:S(2)}, u32[]{:S(2)}) collective-permute-start(f32[1,1,128,256]{3,2,1,0:T(8,128)} %get-tuple-element.9), channel_id=1, source_target_pairs={{0,3},{1,0},{2,1},{3,2},{4,7},{5,4},{6,5},{7,6},{8,11},{9,8},{10,9... | collective-permute-start | bytes 393224 | tf_op jit(solution)/shard_map/ppermute | solution.py:20
  150.5 11.9 %collective-permute-start.13 = (f32[1,1,128,256]{3,2,1,0:T(8,128)S(1)}, f32[1,1,128,256]{3,2,1,0:T(8,128)S(1)}, u32[]{:S(2)}, u32[]{:S(2)}) collective-permute-start(f32[1,1,128,256]{3,2,1,0:T(8,128)S(1)} %get-tuple-element.7), channel_id=1, source_target_pairs={{0,1},{1,2},{2,3},{3,0},{4,5},{5,6},{6,7},{7,4},{8,9},{9,10},{10,1... | collective-permute-start | bytes 393224 | tf_op jit(solution)/shard_map/ppermute | solution.py:20
  157.2 28.8 %copy-start.6 = (s32[16]{0:T(128)S(1)}, s32[16]{0:T(128)}, u32[]{:S(2)}) copy-start(s32[16]{0:T(128)} %param.13) | copy-start | bytes 196
  157.2 29.4 %copy-start.7 = (f32[16]{0:T(128)S(1)}, f32[16]{0:T(128)}, u32[]{:S(2)}) copy-start(f32[16]{0:T(128)} %param.12) | copy-start | bytes 196
  157.2 11.1 %collective-permute-start.14 = (f32[1,1,128,256]{3,2,1,0:T(8,128)S(1)}, f32[1,1,128,256]{3,2,1,0:T(8,128)S(1)}, u32[]{:S(2)}, u32[]{:S(2)}) collective-permute-start(f32[1,1,128,256]{3,2,1,0:T(8,128)S(1)} %get-tuple-element.7), channel_id=1, source_target_pairs={{0,2},{1,3},{2,0},{3,1},{4,6},{5,7},{6,4},{7,5},{8,10},{9,11},{10,... | collective-permute-start | bytes 393224 | tf_op jit(solution)/shard_map/ppermute | solution.py:20
  158.9 12.5 %collective-permute-start.6 = (f32[1,2,256,256]{3,2,1,0:T(8,128)S(1)}, f32[1,2,256,256]{3,2,1,0:T(8,128)S(1)}, u32[]{:S(2)}, u32[]{:S(2)}) collective-permute-start(f32[1,2,256,256]{3,2,1,0:T(8,128)S(1)} %bitcast.104), channel_id=1, source_target_pairs={{0,8},{4,12},{8,0},{12,4},{1,9},{5,13},{9,1},{13,5},{2,10},{6,14},... | collective-permute-start | bytes 1572872 | tf_op jit(solution)/shard_map/ppermute | solution.py:278
  159.3 11.7 %collective-permute-start.15 = (f32[1,1,128,256]{3,2,1,0:T(8,128)S(1)}, f32[1,1,128,256]{3,2,1,0:T(8,128)S(1)}, u32[]{:S(2)}, u32[]{:S(2)}) collective-permute-start(f32[1,1,128,256]{3,2,1,0:T(8,128)S(1)} %get-tuple-element.7), channel_id=1, source_target_pairs={{0,3},{1,0},{2,1},{3,2},{4,7},{5,4},{6,5},{7,6},{8,11},{9,8},{10,9... | collective-permute-start | bytes 393224 | tf_op jit(solution)/shard_map/ppermute | solution.py:20
  171.0 13.9 %collective-permute-start.16 = (f32[1,2,256,256]{3,2,1,0:T(8,128)S(1)}, f32[1,2,256,256]{3,2,1,0:T(8,128)S(1)}, u32[]{:S(2)}, u32[]{:S(2)}) collective-permute-start(f32[1,2,256,256]{3,2,1,0:T(8,128)S(1)} %bitcast.101), channel_id=1, source_target_pairs={{0,8},{4,12},{8,0},{12,4},{1,9},{5,13},{9,1},{13,5},{2,10},{6,14},... | collective-permute-start | bytes 1572872 | tf_op jit(solution)/shard_map/ppermute | solution.py:278
  171.5 16.4 %collective-permute-start.7 = (f32[2,2,256,256]{3,2,1,0:T(8,128)S(1)}, f32[2,2,256,256]{3,2,1,0:T(8,128)}, u32[]{:S(2)}, u32[]{:S(2)}) collective-permute-start(f32[2,2,256,256]{3,2,1,0:T(8,128)S(1)} %pad_maximum_fusion.2), channel_id=1, source_target_pairs={{0,4},{4,0},{8,12},{12,8},{1,5},{5,1},{9,13},{13,9},{2,6},{6,2},{1... | collective-permute-start | bytes 3145736 | tf_op jit(solution)/shard_map/ppermute | solution.py:278
  186.0 3.4 %collective-permute-start.17 = (f32[2,2,256,256]{3,2,1,0:T(8,128)}, f32[2,2,256,256]{3,2,1,0:T(8,128)}, u32[]{:S(2)}, u32[]{:S(2)}) collective-permute-start(f32[2,2,256,256]{3,2,1,0:T(8,128)} %pad_maximum_fusion.3), channel_id=1, source_target_pairs={{0,4},{4,0},{8,12},{12,8},{1,5},{5,1},{9,13},{13,9},{2,6},{6,2},{1... | collective-permute-start | bytes 3145736 | tf_op jit(solution)/shard_map/ppermute | solution.py:278
  (4 other events, 13.8 us)
Sparse Core Ops, SparseCore 0:
  9.6 35.3 all-gather.4
  47.1 31.6 all-gather.2

commit v4 on v3

--- a/solution.py
+++ b/solution.py
@@ -296,14 +296,12 @@
 
 
 def on_device(mode_basis, onsite, onsite_cols, coupling, coupling_cols, energies, owner):
-    halves = [mode_basis[:, :, : M // 2], mode_basis[:, :, M // 2 :]]
-    own = [lax.all_gather(half, "orb", axis=1, tiled=True) for half in halves]
-    following = [
-        jnp.concatenate([all_rows[1:], shifted(all_rows[:1], "slab", -1)], 0) for all_rows in own
-    ]
-    onsite_part = jnp.concatenate(
-        [project(onsite, onsite_cols, mode_basis, half) for half in own], -1
-    )
+    own_all = lax.all_gather(mode_basis, "orb", axis=1, tiled=True)
+    following = []
+    for first in (0, M // 2):
+        half = own_all[:, :, first : first + M // 2]
+        following.append(jnp.concatenate([half[1:], shifted(half[:1], "slab", -1)], 0))
+    onsite_part = project(onsite, onsite_cols, mode_basis, own_all)
     hamil = share(onsite_part)
     coupling_part = jnp.concatenate(
         [project(coupling, coupling_cols, mode_basis, half) for half in following], -1

time: 286 us -> 261 us (0.913)
  local copies, waits for them, and re-layouts: 21.9 us -> 13.8 us
  waiting for transfers between devices: 104 us -> 99.2 us
  matrix products: 22.1 us -> 18.6 us
  starting transfers between devices: 25.7 us -> 22.7 us
    all_gather x2 -> x1, waiting for transfers between devices: 64.3 us -> 58.4 us  [on_device(): own_all = lax.all_gather(mode_basis, 'orb', axis=1, tiled=True)]
    ppermute x14, starting transfers between devices: 24.7 us -> 19.8 us  [shifted(): lax.ppermute(array, axis, [(i, (i + by) % size) for i in range(size)])]
    gather x8 -> x7, local copies, waits for them, and re-layouts: 13.7 us -> 9.48 us  [pick_blocks(): return table[index]]
    dot_general x4 -> x3, matrix products: 20.6 us -> 17.3 us  [project(): jnp.einsum('scbrk,sbkm->scbrm', shaped, chosen, preferred_element_type=jn...]
  transfers between devices with their start and end apart: 20 -> 19, of which waited for: 11 -> 9; matrix products, arithmetic and copies ran while one was open for 14% -> 13% of each run, Pallas kernels for 0% -> 0%
where the time goes in v4:
time: 261 us; the launch traced here: 259 us
  waiting for transfers between devices  99.2 us (38%)
  Pallas kernels  83.5 us (32%)
  starting transfers between devices  22.7 us (9%)
  matrix products  18.6 us (7%)
  between operations  14.3 us (5%)
  local copies, waits for them, and re-layouts  13.8 us (5%)
  other arithmetic  6.57 us (3%)
    pallas_call x1, Pallas kernels, sweep_one(): pl.pallas_call(sweep_kernel, out_shape=(jax.ShapeDtypeStruct((2, M, M), j...  83.5 us
    all_gather x1, waiting for transfers between devices, on_device(): own_all = lax.all_gather(mode_basis, 'orb', axis=1, tiled=True)  58.4 us
    ppermute x14, waiting for transfers between devices, shifted(): lax.ppermute(array, axis, [(i, (i + by) % size) for i in range(size)])  28.8 us
    ppermute x14, starting transfers between devices, shifted(): lax.ppermute(array, axis, [(i, (i + by) % size) for i in range(size)])  19.8 us
    dot_general x3, matrix products, project(): jnp.einsum('scbrk,sbkm->scbrm', shaped, chosen, preferred_element_type=jn...  17.3 us
    ppermute x4, waiting for transfers between devices, share(): other = lax.ppermute(blocks, 'slab', [(i, i ^ bit) for i in range(slabs)])  11.4 us
    gather x7, local copies, waits for them, and re-layouts, pick_blocks(): return table[index]  9.48 us
  transfers between devices with their start and end apart: 19, of which 9 were waited for; matrix products, arithmetic and copies ran while one was open for 13% of the time, Pallas kernels for 0%

profile of v4, /device:TPU:0, one launch (start us, length us, event | category | flops | bytes accessed | tf_op | source)
XLA Modules:
  0.0 258.8 jit_solution(11143009640163267756)
XLA Ops:
  8.7 58.4 %all-gather.2.cloned.1.call-done = bf16[1,5120,256]{2,1,0:T(8,128)(2,1)} async-done(((bf16[1,1280,256]{2,1,0:T(8,128)(2,1)}), bf16[1,5120,256]{2,1,0:T(8,128)(2,1)}) %all-gather.2.cloned.1.call-update) | async-done | bytes 2621456 | tf_op jit(solution)/shard_map/all_gather | solution.py:299
  67.1 3.5 %fusion.39 = (bf16[1,5120,128]{2,1,0:T(8,128)(2,1)}, bf16[1,5120,128]{2,1,0:T(8,128)(2,1)}) fusion(bf16[1,5120,256]{2,1,0:T(8,128)(2,1)} %all-gather.2.cloned.1.call-done), kind=kLoop, calls=%fused_computation.65 | loop fusion | bytes 5242880 | tf_op jit(solution)/shard_map/slice | solution.py:302
  71.5 3.2 %gather_fusion = bf16[64,160,256]{2,1,0:T(8,128)(2,1)} fusion(bf16[1,32,160,256]{3,2,1,0:T(8,128)(2,1)S(1)} %bitcast.82, s32[64]{0:T(128)S(1)} %reshape.115), kind=kCustom, calls=%fused_computation | custom fusion | bytes 10486272 | tf_op jit(solution)/shard_map/vmap()/gather | solution.py:227
  74.7 6.3 %fusion.9 = bf16[1,2,8,160,256]{4,3,1,2,0:T(8,128)(2,1)S(1)} fusion(bf16[8,1280,256,1]{2,1,3,0:T(8,128)(2,1)} %bitcast.84, bf16[2,8,160,1280]{3,2,1,0:T(8,128)(2,1)} %bitcast.100), kind=kOutput, calls=%fused_computation.12 | convolution fusion | flops 1678376960 | bytes 13107200 | tf_op jit(solution)/shard_map/scbrk,sbkm->scbrm/dot_general | solution.py:238
  82.7 1.4 collective-permute-start.2
  84.1 1.9 collective-permute-start
  86.1 2.1 collective-permute-done.2
  88.2 7.5 %collective-permute-done.1 = f32[1,1,128,256]{3,2,1,0:T(8,128)S(1)} collective-permute-done((f32[1,1,128,256]{3,2,1,0:T(8,128)S(1)}, f32[1,1,128,256]{3,2,1,0:T(8,128)S(1)}, u32[]{:S(2)}, u32[]{:S(2)}) %collective-permute-start.1) | collective-permute-done | bytes 131104 | tf_op jit(solution)/shard_map/ppermute | solution.py:20
  96.6 3.7 %gather_fusion.2 = bf16[64,160,128]{2,1,0:T(8,128)(2,1)} fusion(bf16[1,32,160,128]{3,2,1,0:T(8,128)(2,1)} %bitcast.32, s32[64]{0:T(128)S(1)} %reshape.123), kind=kCustom, calls=%fused_computation.2 | custom fusion | bytes 5243392 | tf_op jit(solution)/shard_map/vmap()/gather | solution.py:227
  100.3 5.5 %fusion.18 = bf16[1,2,8,160,128]{4,3,1,2,0:T(8,128)(2,1)S(1)} fusion(bf16[8,1280,128,1]{2,1,3,0:T(8,128)(2,1)} %bitcast.93, bf16[2,8,160,1280]{3,2,1,0:T(8,128)(2,1)} %bitcast.101), kind=kOutput, calls=%fused_computation.15 | convolution fusion | flops 839188480 | bytes 9830400 | tf_op jit(solution)/shard_map/scbrk,sbkm->scbrm/dot_general | solution.py:238
  106.3 2.4 gather_fusion.1
  108.7 5.5 %fusion.21 = bf16[1,2,8,160,128]{4,3,1,2,0:T(8,128)(2,1)S(1)} fusion(bf16[8,1280,128,1]{2,1,3,0:T(8,128)(2,1)} %bitcast.92, bf16[2,8,160,1280]{3,2,1,0:T(8,128)(2,1)} %bitcast.102), kind=kOutput, calls=%fused_computation.16 | convolution fusion | flops 839188480 | bytes 9830400 | tf_op jit(solution)/shard_map/scbrk,sbkm->scbrm/dot_general | solution.py:238
  114.9 3.1 %collective-permute-start.12 = (f32[1,1,128,256]{3,2,1,0:T(8,128)S(1)}, f32[1,1,128,256]{3,2,1,0:T(8,128)S(1)}, u32[]{:S(2)}, u32[]{:S(2)}) collective-permute-start(f32[1,1,128,256]{3,2,1,0:T(8,128)S(1)} %get-tuple-element.13), channel_id=1, source_target_pairs={{0,3},{1,0},{2,1},{3,2},{4,7},{5,4},{6,5},{7,6},{8,11},{9,8},{10,9... | collective-permute-start | bytes 393224 | tf_op jit(solution)/shard_map/ppermute | solution.py:20
  118.9 2.0 collective-permute-start.4
  120.9 2.9 %collective-permute-start.5 = (f32[1,1,128,256]{3,2,1,0:T(8,128)S(1)}, f32[1,1,128,256]{3,2,1,0:T(8,128)S(1)}, u32[]{:S(2)}, u32[]{:S(2)}) collective-permute-start(f32[1,1,128,256]{3,2,1,0:T(8,128)S(1)} %get-tuple-element.9), channel_id=1, source_target_pairs={{0,3},{1,0},{2,1},{3,2},{4,7},{5,4},{6,5},{7,6},{8,11},{9,8},{10,9... | collective-permute-start | bytes 393224 | tf_op jit(solution)/shard_map/ppermute | solution.py:20
  123.9 10.7 %collective-permute-done.11 = f32[1,1,128,256]{3,2,1,0:T(8,128)S(1)} collective-permute-done((f32[1,1,128,256]{3,2,1,0:T(8,128)S(1)}, f32[1,1,128,256]{3,2,1,0:T(8,128)S(1)}, u32[]{:S(2)}, u32[]{:S(2)}) %collective-permute-start.11) | collective-permute-done | bytes 131104 | tf_op jit(solution)/shard_map/ppermute | solution.py:20
  135.9 2.9 %collective-permute-done.4 = f32[1,1,128,256]{3,2,1,0:T(8,128)S(1)} collective-permute-done((f32[1,1,128,256]{3,2,1,0:T(8,128)S(1)}, f32[1,1,128,256]{3,2,1,0:T(8,128)S(1)}, u32[]{:S(2)}, u32[]{:S(2)}) %collective-permute-start.4) | collective-permute-done | bytes 131104 | tf_op jit(solution)/shard_map/ppermute | solution.py:20
  140.1 3.8 %collective-permute-start.15 = (f32[1,1,128,256]{3,2,1,0:T(8,128)S(1)}, f32[1,1,128,256]{3,2,1,0:T(8,128)S(1)}, u32[]{:S(2)}, u32[]{:S(2)}) collective-permute-start(f32[1,1,128,256]{3,2,1,0:T(8,128)S(1)} %get-tuple-element.7), channel_id=1, source_target_pairs={{0,3},{1,0},{2,1},{3,2},{4,7},{5,4},{6,5},{7,6},{8,11},{9,8},{10,9... | collective-permute-start | bytes 393224 | tf_op jit(solution)/shard_map/ppermute | solution.py:20
  143.9 4.5 %collective-permute-done.14 = f32[1,1,128,256]{3,2,1,0:T(8,128)S(1)} collective-permute-done((f32[1,1,128,256]{3,2,1,0:T(8,128)S(1)}, f32[1,1,128,256]{3,2,1,0:T(8,128)S(1)}, u32[]{:S(2)}, u32[]{:S(2)}) %collective-permute-start.14) | collective-permute-done | bytes 131104 | tf_op jit(solution)/shard_map/ppermute | solution.py:20
  149.6 1.6 collective-permute-start.16
  151.2 2.7 %collective-permute-done.6 = f32[1,2,256,256]{3,2,1,0:T(8,128)S(1)} collective-permute-done((f32[1,2,256,256]{3,2,1,0:T(8,128)S(1)}, f32[1,2,256,256]{3,2,1,0:T(8,128)S(1)}, u32[]{:S(2)}, u32[]{:S(2)}) %collective-permute-start.6) | collective-permute-done | bytes 524320 | tf_op jit(solution)/shard_map/ppermute | solution.py:278
  154.0 8.7 %collective-permute-done.16 = f32[1,2,256,256]{3,2,1,0:T(8,128)S(1)} collective-permute-done((f32[1,2,256,256]{3,2,1,0:T(8,128)S(1)}, f32[1,2,256,256]{3,2,1,0:T(8,128)S(1)}, u32[]{:S(2)}, u32[]{:S(2)}) %collective-permute-start.16) | collective-permute-done | bytes 524320 | tf_op jit(solution)/shard_map/ppermute | solution.py:278
  167.0 1.4 pad_maximum_fusion.1.hopping_ref
  168.4 83.5 %shard_map.86 = (f32[2,256,256]{2,1,0:T(8,128)}, f32[4]{0:T(128)}) custom-call(f32[1]{0:T(128)} %bitcast.energy_ref, s32[4]{0:T(128)S(1)} %fusion.38.places_ref, f32[4,2,256,256]{3,2,1,0:T(8,128)S(1)} %pad_maximum_fusion.hamil_ref, f32[4,2,256,256]{3,2,1,0:T(8,128)S(1)} %pad_maximum_fusion.1.hopping_ref), custom_call_target="tpu_custom_call" | custom-call | tf_op jit(solution)/shard_map/pallas_call | solution.py:199
  (65 shorter events, 15.4 us)
Async XLA Ops:
  7.2 59.9 %all-gather.2.cloned.1.call-start = ((), (), s32[]{:S(2)}) async-start(), calls=%async_computation | async-start | bytes 3276800 | tf_op jit(solution)/shard_map/all_gather | solution.py:299
  67.1 4.4 %copy-start = (bf16[1,5120,256]{2,1,0:T(8,128)(2,1)S(1)}, bf16[1,5120,256]{2,1,0:T(8,128)(2,1)}, u32[]{:S(2)}) copy-start(bf16[1,5120,256]{2,1,0:T(8,128)(2,1)} %all-gather.2.cloned.1.call-done) | copy-start | bytes 7864324
  70.6 26.0 %collective-permute-start.9 = (bf16[1,5120,128]{2,1,0:T(8,128)(2,1)}, bf16[1,5120,128]{2,1,0:T(8,128)(2,1)}, u32[]{:S(2)}, u32[]{:S(2)}) collective-permute-start(bf16[1,5120,128]{2,1,0:T(8,128)(2,1)} %get-tuple-element.11), channel_id=1, source_target_pairs={{0,12},{4,0},{8,4},{12,8},{1,13},{5,1},{9,5},{13,9},{2,14},{6,2},{... | collective-permute-start | bytes 3932168 | tf_op jit(solution)/shard_map/ppermute | solution.py:20
  81.0 1.1 copy-start.1
  81.1 25.2 %collective-permute-start.8 = (bf16[1,5120,128]{2,1,0:T(8,128)(2,1)}, bf16[1,5120,128]{2,1,0:T(8,128)(2,1)S(1)}, u32[]{:S(2)}, u32[]{:S(2)}) collective-permute-start(bf16[1,5120,128]{2,1,0:T(8,128)(2,1)} %get-tuple-element.10), channel_id=1, source_target_pairs={{0,12},{4,0},{8,4},{12,8},{1,13},{5,1},{9,5},{13,9},{2,14},{6,2},{... | collective-permute-start | bytes 3932168 | tf_op jit(solution)/shard_map/ppermute | solution.py:20
  82.7 5.5 %collective-permute-start.2 = (f32[1,1,128,256]{3,2,1,0:T(8,128)S(1)}, f32[1,1,128,256]{3,2,1,0:T(8,128)S(1)}, u32[]{:S(2)}, u32[]{:S(2)}) collective-permute-start(f32[1,1,128,256]{3,2,1,0:T(8,128)S(1)} %get-tuple-element.16), channel_id=1, source_target_pairs={{0,3},{1,0},{2,1},{3,2},{4,7},{5,4},{6,5},{7,6},{8,11},{9,8},{10,9... | collective-permute-start | bytes 393224 | tf_op jit(solution)/shard_map/ppermute | solution.py:20
  84.1 11.6 %collective-permute-start.1 = (f32[1,1,128,256]{3,2,1,0:T(8,128)S(1)}, f32[1,1,128,256]{3,2,1,0:T(8,128)S(1)}, u32[]{:S(2)}, u32[]{:S(2)}) collective-permute-start(f32[1,1,128,256]{3,2,1,0:T(8,128)S(1)} %get-tuple-element.17), channel_id=1, source_target_pairs={{0,2},{1,3},{2,0},{3,1},{4,6},{5,7},{6,4},{7,5},{8,10},{9,11},{10,... | collective-permute-start | bytes 393224 | tf_op jit(solution)/shard_map/ppermute | solution.py:20
  84.1 11.6 %collective-permute-start = (f32[1,1,128,256]{3,2,1,0:T(8,128)S(1)}, f32[1,1,128,256]{3,2,1,0:T(8,128)S(1)}, u32[]{:S(2)}, u32[]{:S(2)}) collective-permute-start(f32[1,1,128,256]{3,2,1,0:T(8,128)S(1)} %get-tuple-element.15), channel_id=1, source_target_pairs={{0,1},{1,2},{2,3},{3,0},{4,5},{5,6},{6,7},{7,4},{8,9},{9,10},{10,1... | collective-permute-start | bytes 393224 | tf_op jit(solution)/shard_map/ppermute | solution.py:20
  95.8 25.1 %collective-permute-start.3 = (f32[1,1,128,256]{3,2,1,0:T(8,128)S(1)}, f32[1,1,128,256]{3,2,1,0:T(8,128)S(1)}, u32[]{:S(2)}, u32[]{:S(2)}) collective-permute-start(f32[1,1,128,256]{3,2,1,0:T(8,128)S(1)} %get-tuple-element.9), channel_id=1, source_target_pairs={{0,1},{1,2},{2,3},{3,0},{4,5},{5,6},{6,7},{7,4},{8,9},{9,10},{10,1... | collective-permute-start | bytes 393224 | tf_op jit(solution)/shard_map/ppermute | solution.py:20
  114.9 8.9 %collective-permute-start.12 = (f32[1,1,128,256]{3,2,1,0:T(8,128)S(1)}, f32[1,1,128,256]{3,2,1,0:T(8,128)S(1)}, u32[]{:S(2)}, u32[]{:S(2)}) collective-permute-start(f32[1,1,128,256]{3,2,1,0:T(8,128)S(1)} %get-tuple-element.13), channel_id=1, source_target_pairs={{0,3},{1,0},{2,1},{3,2},{4,7},{5,4},{6,5},{7,6},{8,11},{9,8},{10,9... | collective-permute-start | bytes 393224 | tf_op jit(solution)/shard_map/ppermute | solution.py:20
  118.0 16.6 %collective-permute-start.11 = (f32[1,1,128,256]{3,2,1,0:T(8,128)S(1)}, f32[1,1,128,256]{3,2,1,0:T(8,128)S(1)}, u32[]{:S(2)}, u32[]{:S(2)}) collective-permute-start(f32[1,1,128,256]{3,2,1,0:T(8,128)S(1)} %get-tuple-element.14), channel_id=1, source_target_pairs={{0,2},{1,3},{2,0},{3,1},{4,6},{5,7},{6,4},{7,5},{8,10},{9,11},{10,... | collective-permute-start | bytes 393224 | tf_op jit(solution)/shard_map/ppermute | solution.py:20
  118.9 15.6 %collective-permute-start.10 = (f32[1,1,128,256]{3,2,1,0:T(8,128)S(1)}, f32[1,1,128,256]{3,2,1,0:T(8,128)S(1)}, u32[]{:S(2)}, u32[]{:S(2)}) collective-permute-start(f32[1,1,128,256]{3,2,1,0:T(8,128)S(1)} %get-tuple-element.12), channel_id=1, source_target_pairs={{0,1},{1,2},{2,3},{3,0},{4,5},{5,6},{6,7},{7,4},{8,9},{9,10},{10,1... | collective-permute-start | bytes 393224 | tf_op jit(solution)/shard_map/ppermute | solution.py:20
  118.9 19.8 %collective-permute-start.4 = (f32[1,1,128,256]{3,2,1,0:T(8,128)S(1)}, f32[1,1,128,256]{3,2,1,0:T(8,128)S(1)}, u32[]{:S(2)}, u32[]{:S(2)}) collective-permute-start(f32[1,1,128,256]{3,2,1,0:T(8,128)S(1)} %get-tuple-element.9), channel_id=1, source_target_pairs={{0,2},{1,3},{2,0},{3,1},{4,6},{5,7},{6,4},{7,5},{8,10},{9,11},{10,... | collective-permute-start | bytes 393224 | tf_op jit(solution)/shard_map/ppermute | solution.py:20
  120.9 18.0 %collective-permute-start.5 = (f32[1,1,128,256]{3,2,1,0:T(8,128)S(1)}, f32[1,1,128,256]{3,2,1,0:T(8,128)S(1)}, u32[]{:S(2)}, u32[]{:S(2)}) collective-permute-start(f32[1,1,128,256]{3,2,1,0:T(8,128)S(1)} %get-tuple-element.9), channel_id=1, source_target_pairs={{0,3},{1,0},{2,1},{3,2},{4,7},{5,4},{6,5},{7,6},{8,11},{9,8},{10,9... | collective-permute-start | bytes 393224 | tf_op jit(solution)/shard_map/ppermute | solution.py:20
  134.6 9.3 %collective-permute-start.13 = (f32[1,1,128,256]{3,2,1,0:T(8,128)S(1)}, f32[1,1,128,256]{3,2,1,0:T(8,128)S(1)}, u32[]{:S(2)}, u32[]{:S(2)}) collective-permute-start(f32[1,1,128,256]{3,2,1,0:T(8,128)S(1)} %get-tuple-element.7), channel_id=1, source_target_pairs={{0,1},{1,2},{2,3},{3,0},{4,5},{5,6},{6,7},{7,4},{8,9},{9,10},{10,1... | collective-permute-start | bytes 393224 | tf_op jit(solution)/shard_map/ppermute | solution.py:20
  138.8 25.0 %copy-start.2 = (s32[16]{0:T(128)S(1)}, s32[16]{0:T(128)}, u32[]{:S(2)}) copy-start(s32[16]{0:T(128)} %param.13) | copy-start | bytes 196
  138.8 25.6 %copy-start.3 = (f32[16]{0:T(128)S(1)}, f32[16]{0:T(128)}, u32[]{:S(2)}) copy-start(f32[16]{0:T(128)} %param.12) | copy-start | bytes 196
  138.8 9.7 %collective-permute-start.14 = (f32[1,1,128,256]{3,2,1,0:T(8,128)S(1)}, f32[1,1,128,256]{3,2,1,0:T(8,128)S(1)}, u32[]{:S(2)}, u32[]{:S(2)}) collective-permute-start(f32[1,1,128,256]{3,2,1,0:T(8,128)S(1)} %get-tuple-element.7), channel_id=1, source_target_pairs={{0,2},{1,3},{2,0},{3,1},{4,6},{5,7},{6,4},{7,5},{8,10},{9,11},{10,... | collective-permute-start | bytes 393224 | tf_op jit(solution)/shard_map/ppermute | solution.py:20
  138.9 14.9 %collective-permute-start.6 = (f32[1,2,256,256]{3,2,1,0:T(8,128)S(1)}, f32[1,2,256,256]{3,2,1,0:T(8,128)S(1)}, u32[]{:S(2)}, u32[]{:S(2)}) collective-permute-start(f32[1,2,256,256]{3,2,1,0:T(8,128)S(1)} %bitcast.89), channel_id=1, source_target_pairs={{0,8},{4,12},{8,0},{12,4},{1,9},{5,13},{9,1},{13,5},{2,10},{6,14},... | collective-permute-start | bytes 1572872 | tf_op jit(solution)/shard_map/ppermute | solution.py:278
  140.1 9.5 %collective-permute-start.15 = (f32[1,1,128,256]{3,2,1,0:T(8,128)S(1)}, f32[1,1,128,256]{3,2,1,0:T(8,128)S(1)}, u32[]{:S(2)}, u32[]{:S(2)}) collective-permute-start(f32[1,1,128,256]{3,2,1,0:T(8,128)S(1)} %get-tuple-element.7), channel_id=1, source_target_pairs={{0,3},{1,0},{2,1},{3,2},{4,7},{5,4},{6,5},{7,6},{8,11},{9,8},{10,9... | collective-permute-start | bytes 393224 | tf_op jit(solution)/shard_map/ppermute | solution.py:20
  149.6 13.1 %collective-permute-start.16 = (f32[1,2,256,256]{3,2,1,0:T(8,128)S(1)}, f32[1,2,256,256]{3,2,1,0:T(8,128)S(1)}, u32[]{:S(2)}, u32[]{:S(2)}) collective-permute-start(f32[1,2,256,256]{3,2,1,0:T(8,128)S(1)} %bitcast.86), channel_id=1, source_target_pairs={{0,8},{4,12},{8,0},{12,4},{1,9},{5,13},{9,1},{13,5},{2,10},{6,14},... | collective-permute-start | bytes 1572872 | tf_op jit(solution)/shard_map/ppermute | solution.py:278
  153.9 11.7 %collective-permute-start.7 = (f32[2,2,256,256]{3,2,1,0:T(8,128)S(1)}, f32[2,2,256,256]{3,2,1,0:T(8,128)}, u32[]{:S(2)}, u32[]{:S(2)}) collective-permute-start(f32[2,2,256,256]{3,2,1,0:T(8,128)S(1)} %pad_maximum_fusion.2), channel_id=1, source_target_pairs={{0,4},{4,0},{8,12},{12,8},{1,5},{5,1},{9,13},{13,9},{2,6},{6,2},{1... | collective-permute-start | bytes 3145736 | tf_op jit(solution)/shard_map/ppermute | solution.py:278
  163.7 3.3 %collective-permute-start.17 = (f32[2,2,256,256]{3,2,1,0:T(8,128)}, f32[2,2,256,256]{3,2,1,0:T(8,128)}, u32[]{:S(2)}, u32[]{:S(2)}) collective-permute-start(f32[2,2,256,256]{3,2,1,0:T(8,128)} %pad_maximum_fusion.3), channel_id=1, source_target_pairs={{0,4},{4,0},{8,12},{12,8},{1,5},{5,1},{9,13},{13,9},{2,6},{6,2},{1... | collective-permute-start | bytes 3145736 | tf_op jit(solution)/shard_map/ppermute | solution.py:278
Sparse Core Ops, SparseCore 0:
  9.6 57.4 all-gather.1
